TPU v7x, 32 devices: a whole 2x2x4 slice. The times are simulated.
32 devices in a mesh: leaf: 8 (over z, y), level: 4 (over x, core).
Axes of the slice: x: 2, y: 2, z: 4, core: 2. Of those that a mesh axis runs over, the one named last changes fastest.
Arguments:
- points_x: bfloat16 [256, 16384], P(None, ('leaf', 'level')), may hold values from -6 to 6
- leaf_basis: bfloat16 [32, 512, 256], P(('leaf', 'level')), may hold values from -0.25 to 0.25
- near_tiles: bfloat16 [32, 4, 512, 512], P(('leaf', 'level')), may hold values from -0.25 to 0.25
- near_cols: int32 [32, 4], P(('leaf', 'level')), may hold values from 0 to 11, as said below
- near_count: int32 [32], P(('leaf', 'level')), may hold values from 3 to 4, as said below
- transfer: bfloat16 [2, 256, 256], replicated, may hold values from -0.3125 to 0.3125
- coupling: bfloat16 [6, 2, 256, 256], replicated, may hold values from -0.375 to 0.375
- couple_mask: int32 [6, 8, 2], replicated, may hold values 0 or 1
Outputs:
- kernel_product: bfloat16 [256, 16384], P(None, ('leaf', 'level'))
Inputs may be any that keep to these rules, and one draw needn't show every extreme that they name: Slots 0, 1 and 2 of leaf L name L itself, L - 1 and L + 1 (near_cols 4 + L mod 4, one less, one more); slot 3 names any leaf of the previous, own or next group; some leaf's slot 3 names 0 and some names 11. The live slots of a leaf are its first near_count slots; in every draw some leaf has 3 and some has 4 live slots.
All inputs are finite; a program needn't handle non-finite values.
Results may differ from a plain program's by a relative error of at most 0.015.
Values may be sent and summed in bfloat16 or wider, within the bound.
No kernel may reach another device: no remote copies, remote signals or barrier semaphores. Data moves between devices by JAX's collectives and lax.ppermute only.
A program may use at most 64 MiB of HBM per device.

v0:
```python
from functools import partial

import jax
import jax.numpy as jnp
from jax import lax
from jax.sharding import PartitionSpec as P


def shifted(value, axis, steps):
    count = lax.axis_size(axis)
    leading, last = (max(0, -steps), min(count, count - steps))
    return lax.ppermute(value, axis, [(source, source + steps) for source in range(leading, last)])


def with_halo(block, sides, width):
    for axis, dim in sides:
        count = lax.axis_size(axis)
        forward = [(i, i + 1) for i in range(count - 1)]
        backward = [(target, source) for source, target in forward]
        low = lax.ppermute(
            lax.slice_in_dim(block, block.shape[dim] - width, None, axis=dim), axis, forward
        )
        high = lax.ppermute(lax.slice_in_dim(block, 0, width, axis=dim), axis, backward)
        block = jnp.concatenate([low, block, high], axis=dim)
    return block


def swapped(block, axis, distance):
    count = lax.axis_size(axis)
    route = []
    for low in range(count):
        high = low | 1 << distance
        if high != low and high < count:
            route += [(low, high), (high, low)]
    return lax.ppermute(block, axis, route)


def pair_sum(lower_coef, upper_coef, transfer):
    summed = jnp.dot(lower_coef, transfer[0], preferred_element_type=jnp.float32)
    summed = summed + jnp.dot(upper_coef, transfer[1], preferred_element_type=jnp.float32)
    return summed.astype(jnp.bfloat16)


def down_one(fields, matrix):
    return lax.dot_general(
        fields, matrix, (((1,), (1,)), ((), ())), preferred_element_type=jnp.float32
    )


def partner(coefs, distance):
    return shifted(coefs, "leaf", distance)


def add_tile(column_x, tile_block, running):
    return running + jnp.dot(column_x, tile_block, preferred_element_type=jnp.float32)


def keep_same(running):
    return running


def per_device(
    points_x, leaf_basis, near_tiles, near_cols, near_count, transfer, coupling, couple_mask
):
    group_size = lax.axis_size("level")
    leaf_count = lax.axis_size("leaf")
    group_pos = lax.axis_index("level")
    leaf_pos = lax.axis_index("leaf")
    vectors, points = points_x.shape
    leaf_map = leaf_basis[0]
    slot_count = near_tiles.shape[1]
    levels = coupling.shape[0]
    group_bits = group_size.bit_length() - 1
    leaf_bits = leaf_count.bit_length() - 1
    active = min(levels, leaf_bits + 1)
    leaf_coef = jnp.dot(points_x, leaf_map, preferred_element_type=jnp.float32).astype(jnp.bfloat16)
    padded = with_halo(points_x, (("leaf", 1),), points)
    left_g, own_g, right_g, group_coef = (
        lax.all_gather(padded[:, :points], "level", axis=1, tiled=True),
        lax.all_gather(points_x, "level", axis=1, tiled=True),
        lax.all_gather(padded[:, 2 * points :], "level", axis=1, tiled=True),
        lax.all_gather(leaf_coef[None], "level", axis=0, tiled=True),
    )
    window_x = jnp.concatenate([left_g, own_g, right_g], axis=1)
    level_coefs = [group_coef[member] for member in range(group_size)]
    while len(level_coefs) > 1:
        level_coefs = [
            pair_sum(level_coefs[2 * pair_idx], level_coefs[2 * pair_idx + 1], transfer)
            for pair_idx in range(len(level_coefs) // 2)
        ]
    top_coef = level_coefs[0]
    coarse = [top_coef]
    for level_idx in range(1, active):
        bit_num = level_idx - 1
        current = coarse[-1]
        own_side = leaf_pos >> bit_num & 1
        is_upper = own_side == 1
        partner_coef = swapped(current, "leaf", bit_num)
        lower_coef = jnp.where(is_upper, partner_coef, current)
        upper_coef = jnp.where(is_upper, current, partner_coef)
        coarse.append(pair_sum(lower_coef, upper_coef, transfer))
    couplings = []
    for level_idx in range(active):
        stride = 1 << level_idx
        cluster = leaf_pos >> level_idx
        coupled = jnp.zeros(coarse[level_idx].shape, jnp.float32)
        for pick_idx, offset in enumerate((2, 3)):
            if offset * stride < leaf_count:
                matrix = coupling[level_idx, pick_idx]
                ahead_coef = partner(coarse[level_idx], -offset * stride)
                behind = partner(coarse[level_idx], offset * stride)
                ahead_mask = couple_mask[level_idx, cluster, pick_idx].astype(jnp.float32)
                behind_mask = couple_mask[
                    level_idx, jnp.maximum(cluster - offset, 0), pick_idx
                ].astype(jnp.float32)
                coupled = coupled + ahead_mask * jnp.dot(
                    ahead_coef, matrix, preferred_element_type=jnp.float32
                )
                coupled = coupled + behind_mask * down_one(behind, matrix)
        couplings.append(coupled)
    fields = couplings[active - 1].astype(jnp.bfloat16)
    for level_idx in range(active - 2, -1, -1):
        child_side = leaf_pos >> level_idx & 1
        fields = (down_one(fields, transfer[child_side]) + couplings[level_idx]).astype(
            jnp.bfloat16
        )
    for bit_num in range(group_bits - 1, -1, -1):
        child_side = group_pos >> bit_num & 1
        fields = down_one(fields, transfer[child_side]).astype(jnp.bfloat16)
    far_field = down_one(fields, leaf_map)
    tile_count = near_count[0]
    near_field = far_field
    for slot_idx in range(slot_count):
        column_x = lax.dynamic_slice_in_dim(window_x, near_cols[0, slot_idx] * points, points, 1)
        near_field = lax.cond(
            slot_idx < tile_count,
            partial(add_tile, column_x, near_tiles[0, slot_idx]),
            keep_same,
            near_field,
        )
    return near_field.astype(jnp.bfloat16)


def solution(mesh):
    in_specs = (
        P(None, ("leaf", "level")),
        P(("leaf", "level"), None, None),
        P(("leaf", "level"), None, None, None),
        P(("leaf", "level"), None),
        P(("leaf", "level")),
        P(),
        P(),
        P(),
    )
    out_specs = P(None, ("leaf", "level"))
    return jax.shard_map(
        per_device, mesh=mesh, in_specs=in_specs, out_specs=out_specs, check_vma=False
    )
```

profile of v0, /device:TPU:0, one launch (start us, length us, event | category | flops | bytes accessed | tf_op | source)
XLA Modules:
  0.0 104.6 jit_solution(17333645603289706410)
XLA Ops:
  6.5 5.0 %collective-permute-start.9 = (bf16[256,512]{1,0:T(8,128)(2,1)}, bf16[256,512]{1,0:T(8,128)(2,1)S(1)}, u32[]{:S(2)}, u32[]{:S(2)}) collective-permute-start(bf16[256,512]{1,0:T(8,128)(2,1)} %param.16), channel_id=1, source_target_pairs={{0,4},{4,8},{8,12},{12,16},{16,20},{20,24},{24,28},{1,5},{5,9},{9,... | collective-permute-start | bytes 786440 | tf_op jit(solution)/shard_map/ppermute | solution.py:20
  11.6 5.8 %collective-permute-done.9 = bf16[256,512]{1,0:T(8,128)(2,1)S(1)} collective-permute-done((bf16[256,512]{1,0:T(8,128)(2,1)}, bf16[256,512]{1,0:T(8,128)(2,1)S(1)}, u32[]{:S(2)}, u32[]{:S(2)}) %collective-permute-start.9) | collective-permute-done | bytes 262176 | tf_op jit(solution)/shard_map/ppermute | solution.py:20
  19.0 1.2 %convolution_convert_fusion = bf16[256,256]{1,0:T(8,128)(2,1)S(1)} fusion(bf16[256,512]{1,0:T(8,128)(2,1)} %param.16, bf16[1,512,256]{2,1,0:T(8,128)(2,1)S(1)} %copy-done), kind=kOutput, calls=%fused_computation.44 | convolution fusion | flops 67174400 | bytes 655360 | tf_op jit(solution)/shard_map/dot_general | solution.py:76
  20.2 7.3 %all-gather = bf16[1024,256]{1,0:T(8,128)(2,1)S(1)} all-gather(bf16[256,256]{1,0:T(8,128)(2,1)S(1)} %convolution_convert_fusion), channel_id=2, replica_groups=mesh['leaf'=8,'level'=4] {'level'}, dimensions={0}, use_global_device_ids=true | all-gather | bytes 655360 | tf_op jit(solution)/shard_map/all_gather | solution.py:82
  29.5 2.4 %collective-permute-start = (bf16[256,256]{1,0:T(8,128)(2,1)S(1)}, bf16[256,256]{1,0:T(8,128)(2,1)S(1)}, u32[]{:S(2)}, u32[]{:S(2)}) collective-permute-start(bf16[256,256]{1,0:T(8,128)(2,1)S(1)} %fusion.26), channel_id=1, source_target_pairs={{0,4},{4,0},{8,12},{12,8},{16,20},{20,16},{24,28},{28,24},{1,5},{5... | collective-permute-start | bytes 393224 | tf_op jit(solution)/shard_map/ppermute | solution.py:35
  31.9 4.3 %collective-permute-start.8 = (bf16[256,256]{1,0:T(8,128)(2,1)S(1)}, bf16[256,256]{1,0:T(8,128)(2,1)S(1)}, u32[]{:S(2)}, u32[]{:S(2)}) collective-permute-start(bf16[256,256]{1,0:T(8,128)(2,1)S(1)} %fusion.26), channel_id=1, source_target_pairs={{0,12},{4,16},{8,20},{12,24},{16,28},{1,13},{5,17},{9,21},{13,25},... | collective-permute-start | bytes 393224 | tf_op jit(solution)/shard_map/ppermute | solution.py:12
  36.2 1.3 %collective-permute-start.7 = (bf16[256,256]{1,0:T(8,128)(2,1)S(1)}, bf16[256,256]{1,0:T(8,128)(2,1)S(1)}, u32[]{:S(2)}, u32[]{:S(2)}) collective-permute-start(bf16[256,256]{1,0:T(8,128)(2,1)S(1)} %fusion.26), channel_id=1, source_target_pairs={{12,0},{16,4},{20,8},{24,12},{28,16},{13,1},{17,5},{21,9},{25,13},... | collective-permute-start | bytes 393224 | tf_op jit(solution)/shard_map/ppermute | solution.py:12
  37.5 3.5 %collective-permute-start.6 = (bf16[256,256]{1,0:T(8,128)(2,1)S(1)}, bf16[256,256]{1,0:T(8,128)(2,1)S(1)}, u32[]{:S(2)}, u32[]{:S(2)}) collective-permute-start(bf16[256,256]{1,0:T(8,128)(2,1)S(1)} %fusion.26), channel_id=1, source_target_pairs={{0,8},{4,12},{8,16},{12,20},{16,24},{20,28},{1,9},{5,13},{9,17},{1... | collective-permute-start | bytes 393224 | tf_op jit(solution)/shard_map/ppermute | solution.py:12
  41.0 1.3 %collective-permute-start.5 = (bf16[256,256]{1,0:T(8,128)(2,1)S(1)}, bf16[256,256]{1,0:T(8,128)(2,1)}, u32[]{:S(2)}, u32[]{:S(2)}) collective-permute-start(bf16[256,256]{1,0:T(8,128)(2,1)S(1)} %fusion.26), channel_id=1, source_target_pairs={{8,0},{12,4},{16,8},{20,12},{24,16},{28,20},{9,1},{13,5},{17,9},{2... | collective-permute-start | bytes 393224 | tf_op jit(solution)/shard_map/ppermute | solution.py:12
  51.5 1.3 %collective-permute-start.10 = (bf16[256,512]{1,0:T(8,128)(2,1)S(1)}, bf16[256,512]{1,0:T(8,128)(2,1)S(1)}, u32[]{:S(2)}, u32[]{:S(2)}) collective-permute-start(bf16[256,512]{1,0:T(8,128)(2,1)S(1)} %copy-done.3), channel_id=1, source_target_pairs={{4,0},{8,4},{12,8},{16,12},{20,16},{24,20},{28,24},{5,1},{9,5},{13... | collective-permute-start | bytes 786440 | tf_op jit(solution)/shard_map/ppermute | solution.py:23
  53.2 1.3 %collective-permute-start.3 = (bf16[256,256]{1,0:T(8,128)(2,1)S(1)}, bf16[256,256]{1,0:T(8,128)(2,1)S(1)}, u32[]{:S(2)}, u32[]{:S(2)}) collective-permute-start(bf16[256,256]{1,0:T(8,128)(2,1)S(1)} %fusion.27), channel_id=1, source_target_pairs={{24,0},{28,4},{25,1},{29,5},{26,2},{30,6},{27,3},{31,7}} | collective-permute-start | bytes 393224 | tf_op jit(solution)/shard_map/ppermute | solution.py:12
  54.5 1.1 %convolution_multiply_fusion = f32[256,256]{1,0:T(8,128)S(1)} fusion(bf16[256,256]{1,0:T(8,128)(2,1)S(1)} %collective-permute-done.8, f32[]{:T(128)} %bitcast.23, bf16[6,2,256,256]{3,2,1,0:T(8,128)(2,1)} %param.22), kind=kOutput, calls=%fused_computation.20 | convolution fusion | flops 33619968 | bytes 524800 | tf_op jit(solution)/shard_map/dot_general | solution.py:45
  55.7 8.0 %collective-permute-start.2 = (bf16[256,256]{1,0:T(8,128)(2,1)S(1)}, bf16[256,256]{1,0:T(8,128)(2,1)S(1)}, u32[]{:S(2)}, u32[]{:S(2)}) collective-permute-start(bf16[256,256]{1,0:T(8,128)(2,1)S(1)} %fusion.27), channel_id=1, source_target_pairs={{0,16},{4,20},{8,24},{12,28},{1,17},{5,21},{9,25},{13,29},{2,18},{... | collective-permute-start | bytes 393224 | tf_op jit(solution)/shard_map/ppermute | solution.py:12
  64.8 3.2 %collective-permute-start.4 = (bf16[256,256]{1,0:T(8,128)(2,1)S(1)}, bf16[256,256]{1,0:T(8,128)(2,1)S(1)}, u32[]{:S(2)}, u32[]{:S(2)}) collective-permute-start(bf16[256,256]{1,0:T(8,128)(2,1)S(1)} %fusion.27), channel_id=1, source_target_pairs={{0,24},{4,28},{1,25},{5,29},{2,26},{6,30},{3,27},{7,31}} | collective-permute-start | bytes 393224 | tf_op jit(solution)/shard_map/ppermute | solution.py:12
  69.1 1.3 %collective-permute-start.1 = (bf16[256,256]{1,0:T(8,128)(2,1)S(1)}, bf16[256,256]{1,0:T(8,128)(2,1)S(1)}, u32[]{:S(2)}, u32[]{:S(2)}) collective-permute-start(bf16[256,256]{1,0:T(8,128)(2,1)S(1)} %fusion.27), channel_id=1, source_target_pairs={{16,0},{20,4},{24,8},{28,12},{17,1},{21,5},{25,9},{29,13},{18,2},{... | collective-permute-start | bytes 393224 | tf_op jit(solution)/shard_map/ppermute | solution.py:12
  71.6 1.1 %convolution_multiply_fusion.6 = f32[256,256]{1,0:T(8,128)S(1)} fusion(bf16[256,256]{1,0:T(8,128)(2,1)S(1)} %collective-permute-done.2, f32[]{:T(128)} %bitcast.13, bf16[6,2,256,256]{3,2,1,0:T(8,128)(2,1)} %param.22), kind=kOutput, calls=%fused_computation.28 | convolution fusion | flops 33619968 | bytes 524800 | tf_op jit(solution)/shard_map/dot_general | solution.py:45
  72.7 1.1 %convolution_multiply_fusion.4 = f32[256,256]{1,0:T(8,128)S(1)} fusion(bf16[256,256]{1,0:T(8,128)(2,1)S(1)} %collective-permute-done.4, f32[]{:T(128)} %bitcast.16, bf16[6,2,256,256]{3,2,1,0:T(8,128)(2,1)} %param.22), kind=kOutput, calls=%fused_computation.26 | convolution fusion | flops 33619968 | bytes 524800 | tf_op jit(solution)/shard_map/dot_general | solution.py:45
  73.9 4.3 %collective-permute-done.1 = bf16[256,256]{1,0:T(8,128)(2,1)S(1)} collective-permute-done((bf16[256,256]{1,0:T(8,128)(2,1)S(1)}, bf16[256,256]{1,0:T(8,128)(2,1)S(1)}, u32[]{:S(2)}, u32[]{:S(2)}) %collective-permute-start.1) | collective-permute-done | bytes 131104 | tf_op jit(solution)/shard_map/ppermute | solution.py:12
  78.2 1.2 %fusion.32 = f32[256,256]{1,0:T(8,128)S(1)} fusion(f32[256,256]{1,0:T(8,128)S(1)} %fusion.33, f32[256,256]{1,0:T(8,128)S(1)} %convolution_multiply_fusion.4, f32[256,256]{1,0:T(8,128)S(1)} %convolution_multiply_fusion.5, f32[256,256]{1,0:T(8,128)S(1)} %convolution_multiply_fusion.6, bf16[256,256]{1,0:T(8,128)(2,1)S(1)} %collective-permute-done.1, ...), kind=kOutput, calls=%fused_computation.52 | convolution fusion | flops 67502080 | bytes 1704452 | tf_op jit(solution)/shard_map/dot_general | solution.py:45
  79.5 1.3 %convolution_convert_fusion.2 = bf16[256,256]{1,0:T(8,128)(2,1)S(1)} fusion(f32[256,256]{1,0:T(8,128)S(1)} %fusion.32, f32[256,256]{1,0:T(8,128)S(1)} %convolution_multiply_fusion, f32[256,256]{1,0:T(8,128)S(1)} %convolution_multiply_fusion.1, f32[256,256]{1,0:T(8,128)S(1)} %convolution_multiply_fusion.2, bf16[256,256]{1,0:T(8,128)(2,1)} %collective-permute-done.5, ...), kind=kOutput, calls=%fused_computation.46 | convolution fusion | flops 67567616 | bytes 1573380 | tf_op jit(solution)/shard_map/dot_general | solution.py:45
  81.2 2.3 %constant_dynamic-update-slice_fusion.2 = bf16[256,6144]{1,0:T(8,128)(2,1)} fusion(bf16[256,2048]{1,0:T(8,128)(2,1)} %all-gather.5.cloned.1.call-done), kind=kLoop, calls=%fused_computation.112 | loop fusion | bytes 2097152
  83.5 2.5 %constant_dynamic-update-slice_fusion.1 = bf16[256,6144]{1,0:T(8,128)(2,1)} fusion(bf16[256,6144]{1,0:T(8,128)(2,1)} %constant_dynamic-update-slice_fusion.2, bf16[256,2048]{1,0:T(8,128)(2,1)} %all-gather.7.cloned.1.call-done), kind=kLoop, calls=%fused_computation.111 | loop fusion | bytes 2097152
  86.0 2.4 %all-gather.9.cloned.1.call-done = bf16[256,2048]{1,0:T(8,128)(2,1)} async-done(((bf16[256,512]{1,0:T(8,128)(2,1)}), bf16[256,2048]{1,0:T(8,128)(2,1)}) %all-gather.9.cloned.1.call-update) | async-done | bytes 1048592 | tf_op jit(solution)/shard_map/all_gather | solution.py:81
  88.4 2.3 %constant_dynamic-update-slice_fusion = bf16[256,6144]{1,0:T(8,128)(2,1)} fusion(bf16[256,6144]{1,0:T(8,128)(2,1)} %constant_dynamic-update-slice_fusion.1, bf16[256,2048]{1,0:T(8,128)(2,1)} %all-gather.9.cloned.1.call-done), kind=kLoop, calls=%fused_computation.110 | loop fusion | bytes 2097152 | tf_op jit(solution)/shard_map/concatenate | solution.py:84
  90.7 1.3 %conditional.7 = (f32[256,512]{1,0:T(8,128)S(1)}) conditional(s32[]{:T(128)} %bitcast.5, f32[256,512]{1,0:T(8,128)S(1)} %fusion.30, (bf16[256,6144]{1,0:T(8,128)(2,1)}, bf16[1,4,512,512]{3,2,1,0:T(8,128)(2,1)S(1)}, f32[256,512]{1,0:T(8,128)S(1)}, s32[]{:T(128)}, s32[]{:T(128)}, /*index=5*/s32[]{:T(128)}, s32[]{:T(128)}, s32[]{:T(128)}) %tuple.77), branch_computations={%region_0.1_spmd, %region_1.2_spmd.clone} | conditional | flops 134348800 | bytes 1835054 | solution.py:135
  90.7 1.3 %convolution_add_fusion.1 = f32[256,512]{1,0:T(8,128)S(1)} fusion(f32[256,512]{1,0:T(8,128)S(1)} %get-tuple-element.149, bf16[1,4,512,512]{3,2,1,0:T(8,128)(2,1)S(1)} %get-tuple-element.153, bf16[256,6144]{1,0:T(8,128)(2,1)} %get-tuple-element.150, s32[]{:T(128)S(6)} %select_n.70), kind=kOutput, calls=%fused_computation.5 | convolution fusion | flops 134348800 | bytes 1835012 | tf_op jit(solution)/shard_map/cond/branch_1_fun/dot_general | solution.py:55
  92.0 1.4 %conditional.8 = (f32[256,512]{1,0:T(8,128)S(1)}) conditional(s32[]{:T(128)} %bitcast.4, f32[256,512]{1,0:T(8,128)S(1)} %get-tuple-element.215, (bf16[256,6144]{1,0:T(8,128)(2,1)}, bf16[1,4,512,512]{3,2,1,0:T(8,128)(2,1)S(1)}, f32[256,512]{1,0:T(8,128)S(1)}, s32[]{:T(128)}, s32[]{:T(128)}, /*index=5*/s32[]{:T(128)}, s32[]{:T(128)}, ...), branch_computations={%region_2.3_spmd, %region_3.4_spmd.clone} | conditional | flops 134348800 | bytes 1835054 | solution.py:135
  92.1 1.3 %convolution_add_fusion.2 = f32[256,512]{1,0:T(8,128)S(1)} fusion(f32[256,512]{1,0:T(8,128)S(1)} %get-tuple-element.166, bf16[1,4,512,512]{3,2,1,0:T(8,128)(2,1)S(1)} %get-tuple-element.170, bf16[256,6144]{1,0:T(8,128)(2,1)} %get-tuple-element.167, s32[]{:T(128)S(6)} %select_n.71), kind=kOutput, calls=%fused_computation.10 | convolution fusion | flops 134348800 | bytes 1835012 | tf_op jit(solution)/shard_map/cond/branch_1_fun/dot_general | solution.py:55
  93.4 1.4 %conditional.9 = (f32[256,512]{1,0:T(8,128)S(1)}) conditional(s32[]{:T(128)} %bitcast.3, f32[256,512]{1,0:T(8,128)S(1)} %get-tuple-element.216, (bf16[256,6144]{1,0:T(8,128)(2,1)}, bf16[1,4,512,512]{3,2,1,0:T(8,128)(2,1)S(1)}, f32[256,512]{1,0:T(8,128)S(1)}, s32[]{:T(128)}, s32[]{:T(128)}, /*index=5*/s32[]{:T(128)}, s32[]{:T(128)}, ...), branch_computations={%region_4.5_spmd, %region_5.6_spmd.clone} | conditional | flops 134348800 | bytes 1835054 | solution.py:135
  93.4 1.3 %convolution_add_fusion.3 = f32[256,512]{1,0:T(8,128)S(1)} fusion(f32[256,512]{1,0:T(8,128)S(1)} %get-tuple-element.183, bf16[1,4,512,512]{3,2,1,0:T(8,128)(2,1)S(1)} %get-tuple-element.187, bf16[256,6144]{1,0:T(8,128)(2,1)} %get-tuple-element.184, s32[]{:T(128)S(6)} %select_n.72), kind=kOutput, calls=%fused_computation.15 | convolution fusion | flops 134348800 | bytes 1835012 | tf_op jit(solution)/shard_map/cond/branch_1_fun/dot_general | solution.py:55
  94.8 2.5 %conditional.11 = (f32[256,512]{1,0:T(8,128)S(1)}) conditional(s32[]{:T(128)} %bitcast.2, f32[256,512]{1,0:T(8,128)S(1)} %get-tuple-element.217, (s32[1,4]{1,0:T(1,128)S(1)}, bf16[256,6144]{1,0:T(8,128)(2,1)}, bf16[1,4,512,512]{3,2,1,0:T(8,128)(2,1)S(1)}, f32[256,512]{1,0:T(8,128)S(1)}) %tuple.81), branch_computations={%region_6.7_spmd, %region_7.8_spmd} | conditional | flops 134348800 | bytes 1835074
  96.0 1.3 %convolution_add_fusion = f32[256,512]{1,0:T(8,128)S(1)} fusion(f32[256,512]{1,0:T(8,128)S(1)} %get-tuple-element.108, bf16[1,4,512,512]{3,2,1,0:T(8,128)(2,1)S(1)} %get-tuple-element.111, bf16[256,6144]{1,0:T(8,128)(2,1)} %get-tuple-element.109, s32[]{:T(128)S(6)} %select_n.40), kind=kOutput, calls=%fused_computation | convolution fusion | flops 134348800 | bytes 1835012 | tf_op jit(solution)/shard_map/cond/branch_1_fun/dot_general | solution.py:55
  (48 shorter events, 10.7 us)
Async XLA Ops:
  6.5 12.4 %copy-start = (bf16[1,512,256]{2,1,0:T(8,128)(2,1)S(1)}, bf16[1,512,256]{2,1,0:T(8,128)(2,1)}, u32[]{:S(2)}) copy-start(bf16[1,512,256]{2,1,0:T(8,128)(2,1)} %param.17) | copy-start | bytes 786436
  6.5 22.0 %copy-start.1 = (bf16[2,256,256]{2,1,0:T(8,128)(2,1)S(1)}, bf16[2,256,256]{2,1,0:T(8,128)(2,1)}, u32[]{:S(2)}) copy-start(bf16[2,256,256]{2,1,0:T(8,128)(2,1)} %param.21) | copy-start | bytes 786436
  6.5 74.7 %all-gather.5.cloned.1.call-start = ((), (), s32[]{:S(2)}) async-start(), calls=%async_computation | async-start | bytes 1310720 | tf_op jit(solution)/shard_map/all_gather | solution.py:79
  6.5 10.9 %collective-permute-start.9 = (bf16[256,512]{1,0:T(8,128)(2,1)}, bf16[256,512]{1,0:T(8,128)(2,1)S(1)}, u32[]{:S(2)}, u32[]{:S(2)}) collective-permute-start(bf16[256,512]{1,0:T(8,128)(2,1)} %param.16), channel_id=1, source_target_pairs={{0,4},{4,8},{8,12},{12,16},{16,20},{20,24},{24,28},{1,5},{5,9},{9,... | collective-permute-start | bytes 786440 | tf_op jit(solution)/shard_map/ppermute | solution.py:20
  17.4 0.7 copy-start.4
  18.1 65.4 %all-gather.7.cloned.1.call-start = ((), (), s32[]{:S(2)}) async-start(), calls=%async_computation.1 | async-start | bytes 1310720 | tf_op jit(solution)/shard_map/all_gather | solution.py:80
  18.9 23.4 %copy-start.6 = (s32[1,4]{1,0:T(1,128)S(1)}, s32[1,4]{1,0:T(1,128)}, u32[]{:S(2)}) copy-start(s32[1,4]{1,0:T(1,128)} %param.19) | copy-start | bytes 52
  18.9 24.1 %copy-start.7 = (s32[6,8,2]{1,2,0:T(2,128)S(1)}, s32[6,8,2]{1,2,0:T(2,128)}, u32[]{:S(2)}) copy-start(s32[6,8,2]{1,2,0:T(2,128)} %param.23) | copy-start | bytes 1156
  18.9 69.5 %all-gather.9.cloned.1.call-start = ((), (), s32[]{:S(2)}) async-start(), calls=%async_computation.2 | async-start | bytes 1310720 | tf_op jit(solution)/shard_map/all_gather | solution.py:81
  20.1 31.4 %copy-start.3 = (bf16[256,512]{1,0:T(8,128)(2,1)S(1)}, bf16[256,512]{1,0:T(8,128)(2,1)}, u32[]{:S(2)}) copy-start(bf16[256,512]{1,0:T(8,128)(2,1)} %param.16) | copy-start | bytes 786436
  29.5 22.1 %collective-permute-start = (bf16[256,256]{1,0:T(8,128)(2,1)S(1)}, bf16[256,256]{1,0:T(8,128)(2,1)S(1)}, u32[]{:S(2)}, u32[]{:S(2)}) collective-permute-start(bf16[256,256]{1,0:T(8,128)(2,1)S(1)} %fusion.26), channel_id=1, source_target_pairs={{0,4},{4,0},{8,12},{12,8},{16,20},{20,16},{24,28},{28,24},{1,5},{5... | collective-permute-start | bytes 393224 | tf_op jit(solution)/shard_map/ppermute | solution.py:35
  31.9 21.3 %collective-permute-start.8 = (bf16[256,256]{1,0:T(8,128)(2,1)S(1)}, bf16[256,256]{1,0:T(8,128)(2,1)S(1)}, u32[]{:S(2)}, u32[]{:S(2)}) collective-permute-start(bf16[256,256]{1,0:T(8,128)(2,1)S(1)} %fusion.26), channel_id=1, source_target_pairs={{0,12},{4,16},{8,20},{12,24},{16,28},{1,13},{5,17},{9,21},{13,25},... | collective-permute-start | bytes 393224 | tf_op jit(solution)/shard_map/ppermute | solution.py:12
  36.2 19.5 %collective-permute-start.7 = (bf16[256,256]{1,0:T(8,128)(2,1)S(1)}, bf16[256,256]{1,0:T(8,128)(2,1)S(1)}, u32[]{:S(2)}, u32[]{:S(2)}) collective-permute-start(bf16[256,256]{1,0:T(8,128)(2,1)S(1)} %fusion.26), channel_id=1, source_target_pairs={{12,0},{16,4},{20,8},{24,12},{28,16},{13,1},{17,5},{21,9},{25,13},... | collective-permute-start | bytes 393224 | tf_op jit(solution)/shard_map/ppermute | solution.py:12
  37.5 27.3 %collective-permute-start.6 = (bf16[256,256]{1,0:T(8,128)(2,1)S(1)}, bf16[256,256]{1,0:T(8,128)(2,1)S(1)}, u32[]{:S(2)}, u32[]{:S(2)}) collective-permute-start(bf16[256,256]{1,0:T(8,128)(2,1)S(1)} %fusion.26), channel_id=1, source_target_pairs={{0,8},{4,12},{8,16},{12,20},{16,24},{20,28},{1,9},{5,13},{9,17},{1... | collective-permute-start | bytes 393224 | tf_op jit(solution)/shard_map/ppermute | solution.py:12
  41.0 38.4 %collective-permute-start.5 = (bf16[256,256]{1,0:T(8,128)(2,1)S(1)}, bf16[256,256]{1,0:T(8,128)(2,1)}, u32[]{:S(2)}, u32[]{:S(2)}) collective-permute-start(bf16[256,256]{1,0:T(8,128)(2,1)S(1)} %fusion.26), channel_id=1, source_target_pairs={{8,0},{12,4},{16,8},{20,12},{24,16},{28,20},{9,1},{13,5},{17,9},{2... | collective-permute-start | bytes 393224 | tf_op jit(solution)/shard_map/ppermute | solution.py:12
  51.5 17.6 %collective-permute-start.10 = (bf16[256,512]{1,0:T(8,128)(2,1)S(1)}, bf16[256,512]{1,0:T(8,128)(2,1)S(1)}, u32[]{:S(2)}, u32[]{:S(2)}) collective-permute-start(bf16[256,512]{1,0:T(8,128)(2,1)S(1)} %copy-done.3), channel_id=1, source_target_pairs={{4,0},{8,4},{12,8},{16,12},{20,16},{24,20},{28,24},{5,1},{9,5},{13... | collective-permute-start | bytes 786440 | tf_op jit(solution)/shard_map/ppermute | solution.py:23
  53.2 17.2 %collective-permute-start.3 = (bf16[256,256]{1,0:T(8,128)(2,1)S(1)}, bf16[256,256]{1,0:T(8,128)(2,1)S(1)}, u32[]{:S(2)}, u32[]{:S(2)}) collective-permute-start(bf16[256,256]{1,0:T(8,128)(2,1)S(1)} %fusion.27), channel_id=1, source_target_pairs={{24,0},{28,4},{25,1},{29,5},{26,2},{30,6},{27,3},{31,7}} | collective-permute-start | bytes 393224 | tf_op jit(solution)/shard_map/ppermute | solution.py:12
  55.7 15.9 %collective-permute-start.2 = (bf16[256,256]{1,0:T(8,128)(2,1)S(1)}, bf16[256,256]{1,0:T(8,128)(2,1)S(1)}, u32[]{:S(2)}, u32[]{:S(2)}) collective-permute-start(bf16[256,256]{1,0:T(8,128)(2,1)S(1)} %fusion.27), channel_id=1, source_target_pairs={{0,16},{4,20},{8,24},{12,28},{1,17},{5,21},{9,25},{13,29},{2,18},{... | collective-permute-start | bytes 393224 | tf_op jit(solution)/shard_map/ppermute | solution.py:12
  64.8 8.0 %collective-permute-start.4 = (bf16[256,256]{1,0:T(8,128)(2,1)S(1)}, bf16[256,256]{1,0:T(8,128)(2,1)S(1)}, u32[]{:S(2)}, u32[]{:S(2)}) collective-permute-start(bf16[256,256]{1,0:T(8,128)(2,1)S(1)} %fusion.27), channel_id=1, source_target_pairs={{0,24},{4,28},{1,25},{5,29},{2,26},{6,30},{3,27},{7,31}} | collective-permute-start | bytes 393224 | tf_op jit(solution)/shard_map/ppermute | solution.py:12
  69.1 1.3 %copy-start.5 = (bf16[256,512]{1,0:T(8,128)(2,1)}, bf16[256,512]{1,0:T(8,128)(2,1)S(1)}, u32[]{:S(2)}) copy-start(bf16[256,512]{1,0:T(8,128)(2,1)S(1)} %collective-permute-done.10) | copy-start | bytes 786436
  69.1 9.1 %collective-permute-start.1 = (bf16[256,256]{1,0:T(8,128)(2,1)S(1)}, bf16[256,256]{1,0:T(8,128)(2,1)S(1)}, u32[]{:S(2)}, u32[]{:S(2)}) collective-permute-start(bf16[256,256]{1,0:T(8,128)(2,1)S(1)} %fusion.27), channel_id=1, source_target_pairs={{16,0},{20,4},{24,8},{28,12},{17,1},{21,5},{25,9},{29,13},{18,2},{... | collective-permute-start | bytes 393224 | tf_op jit(solution)/shard_map/ppermute | solution.py:12
  83.5 7.2 %copy-start.2 = (bf16[1,4,512,512]{3,2,1,0:T(8,128)(2,1)S(1)}, bf16[1,4,512,512]{3,2,1,0:T(8,128)(2,1)}, u32[]{:S(2)}) copy-start(bf16[1,4,512,512]{3,2,1,0:T(8,128)(2,1)} %param.18) | copy-start | bytes 6291460
Sparse Core Ops, SparseCore 0:
  18.3 18.8 all-gather.4
  38.7 16.7 all-gather.6
  70.6 17.7 all-gather.8
where the time goes:
time: 105 us
  starting transfers between devices  33 us (31%)
  between operations  21 us (20%)
  matrix products  18.8 us (18%)
  waiting for transfers between devices  13.3 us (13%)
  local copies, waits for them, and re-layouts  9.72 us (9%)
  blocking collectives  7.31 us (7%)
    ppermute x8, starting transfers between devices, shifted(): lax.ppermute(value, axis, [(source, source + steps) for source in range(l...  24.2 us
    dot_general x8, matrix products, down_one(): lax.dot_general(fields, matrix, (((1,), (1,)), ((), ())), preferred_eleme...  7.86 us
    all_gather x1, blocking collectives, per_device(): lax.all_gather(leaf_coef[None], 'level', axis=0, tiled=True)  7.31 us
    ppermute x1, waiting for transfers between devices, with_halo(): lax.ppermute(lax.slice_in_dim(block, block.shape[dim] - width, None, axis...  5.85 us
    unnamed x18, local copies, waits for them, and re-layouts  5.5 us
    dot_general x4, matrix products, add_tile(): jnp.dot(column_x, tile_block, preferred_element_type=jnp.float32)  5.27 us
    ppermute x1, starting transfers between devices, with_halo(): lax.ppermute(lax.slice_in_dim(block, block.shape[dim] - width, None, axis...  5.01 us
    ppermute x8, waiting for transfers between devices, shifted(): lax.ppermute(value, axis, [(source, source + steps) for source in range(l...  4.34 us
  transfers between devices with their start and end apart: 14, of which 3 were waited for; matrix products, arithmetic and copies ran while one was open for 19% of the time, Pallas kernels for 0%

commit v1 on v0

v1 whole, which is shorter than its diff:
```python
from functools import partial

import jax
import jax.numpy as jnp
from jax import lax
from jax.experimental import pallas as pl
from jax.experimental.pallas import tpu as pltpu
from jax.sharding import PartitionSpec as P

VMEM_LIMIT = 32 * 1024 * 1024
F32 = jnp.float32
BF16 = jnp.bfloat16
GROUP = 4


def dot(a, b):
    return jnp.dot(a, b, preferred_element_type=F32)


def dot_t(a, b):
    return lax.dot_general(a, b, (((1,), (1,)), ((), ())), preferred_element_type=F32)


def call(kernel, name, flops, inputs, scalars, outputs, scratch=()):
    shapes = [jax.ShapeDtypeStruct(shape, dtype) for shape, dtype in outputs]
    moved = sum(a.size * a.dtype.itemsize for a in inputs) + sum(
        s.size * s.dtype.itemsize for s in shapes
    )
    return pl.pallas_call(
        kernel,
        out_shape=shapes,
        in_specs=[pl.BlockSpec(memory_space=pltpu.VMEM)] * len(inputs)
        + [pl.BlockSpec(memory_space=pltpu.SMEM)] * len(scalars),
        out_specs=[pl.BlockSpec(memory_space=pltpu.VMEM)] * len(outputs),
        scratch_shapes=list(scratch),
        compiler_params=pltpu.CompilerParams(vmem_limit_bytes=VMEM_LIMIT),
        cost_estimate=pl.CostEstimate(flops=flops, bytes_accessed=moved, transcendentals=0),
        name=name,
    )(*inputs, *scalars)


def up_kernel(bits, x_ref, basis_ref, transfer_ref, *refs):
    *share_refs, w_ref, z_ref = refs
    pos = lax.axis_index("level")
    w = basis_ref[0]
    for bit in range(bits):
        w = dot(w, transfer_ref[pos >> bit & 1]).astype(BF16)
    w_ref[...] = w
    z = dot(x_ref[...], w).astype(BF16)
    rows = z_ref.shape[1]
    for member in range(GROUP):
        z_ref[member] = z[member * rows : (member + 1) * rows]
    for turn, share_ref in enumerate(share_refs):
        share_ref[...] = z_ref[pos ^ turn]


def push_kernel(
    turns, pairs, clusters, own_ref, mate_ref, coupling_ref, transfer_ref, mask_ref, *refs
):
    *push_refs, both_ref, pair_ref = refs
    leaf_pos = lax.axis_index("leaf")
    pair, side = leaf_pos >> 1, leaf_pos & 1
    both_ref[side] = own_ref[...]
    both_ref[1 - side] = mate_ref[...]
    total = dot(both_ref[0], transfer_ref[0]) + dot(both_ref[1], transfer_ref[1])
    pair_ref[...] = total.astype(BF16)

    def term(lev, coef, gap, source, target):
        pick = abs(gap) - 2
        matrix = coupling_ref[lev, pick]
        switch = mask_ref[lev, source if gap > 0 else target, pick].astype(F32)
        return switch * (dot_t(coef, matrix) if gap > 0 else dot(coef, matrix))

    def fill(push_ref, distance, to_side):
        target_pair = pair + distance
        total = None
        if abs(distance) in (2, 3) and clusters[1]:
            coupled = term(1, pair_ref[...], distance, pair, target_pair).astype(BF16)
            total = dot_t(coupled, transfer_ref[to_side])
        for from_side in (0, 1):
            gap = 2 * distance + to_side - from_side
            if abs(gap) in (2, 3) and clusters[0]:
                more = term(
                    0, both_ref[from_side], gap, 2 * pair + from_side, 2 * target_pair + to_side
                )
                total = more if total is None else total + more
        if total is None:
            total = jnp.zeros(push_ref.shape, F32)
        push_ref[...] = total.astype(BF16)

    for turn, push_ref in zip(turns, push_refs):
        for distance in (turn, turn - pairs) if len(turns) < 6 else (turn,):
            target_pair = pair + distance
            inside = jnp.logical_and(target_pair >= 0, target_pair < pairs)
            for to_side in (0, 1):
                @pl.when(jnp.logical_and(inside, side == to_side))
                def _(push_ref=push_ref, distance=distance, to_side=to_side):
                    fill(push_ref, distance, to_side)


def pick_kernel(x_ref, mate_ref, across_ref, corner_ref, left_cols, right_cols, to_left, to_right):
    pos = lax.axis_index("level")
    for cols, out in ((left_cols, to_left), (right_cols, to_right)):
        turn = lax.rem(cols[0, 3], GROUP) ^ pos
        for at, block in enumerate((x_ref, mate_ref, across_ref, corner_ref)):
            @pl.when(turn == at)
            def _(block=block, out=out):
                out[...] = block[...]


def near_kernel(
    x_ref, mate_ref, across_ref, corner_ref, edge_ref, tiles_ref, cols_ref, count_ref, acc_ref
):
    pos = lax.axis_index("level")
    odd = pos & 1
    inner = jnp.logical_or(pos == 1, pos == 2)
    acc = dot(x_ref[...], tiles_ref[0, 0]) + dot(mate_ref[...], tiles_ref[0, 2 - odd])
    beside = jnp.where(inner, corner_ref[...], edge_ref[...])
    acc_ref[...] = acc + dot(beside, tiles_ref[0, 1 + odd])
    col = cols_ref[0, 3]
    turn = lax.rem(col, GROUP) ^ pos
    here = jnp.logical_and(count_ref[0] > 3, col // GROUP == 1)
    for at, block in enumerate((x_ref, mate_ref, across_ref, corner_ref)):
        @pl.when(jnp.logical_and(here, turn == at))
        def _(block=block):
            acc_ref[...] += dot(block[...], tiles_ref[0, 3])


def finish_kernel(
    acc_ref, left_ref, right_ref, tiles_ref, w_ref, field0, field1, field2, field3,
    cols_ref, count_ref, out_ref, total_ref, field_ref
):
    pos = lax.axis_index("level")
    for turn, share_ref in enumerate((field0, field1, field2, field3)):
        field_ref[pos ^ turn] = share_ref[...]
    field = jnp.concatenate([field_ref[member] for member in range(GROUP)], axis=0)
    total_ref[...] = acc_ref[...] + dot_t(field, w_ref[...])
    group = cols_ref[0, 3] // GROUP
    live = count_ref[0] > 3
    for at, block in ((0, left_ref), (2, right_ref)):
        @pl.when(jnp.logical_and(live, group == at))
        def _(block=block):
            total_ref[...] += dot(block[...], tiles_ref[0, 3])
    out_ref[...] = total_ref[...].astype(BF16)


def turned(value, turn):
    return lax.ppermute(value, "level", [(i, i ^ turn) for i in range(GROUP)])


def shifted(value, steps):
    count = lax.axis_size("leaf")
    route = [(i, i + steps) for i in range(count) if 0 <= i + steps < count]
    return lax.ppermute(value, "leaf", route)


def swapped(value, distance):
    count = lax.axis_size("leaf")
    return lax.ppermute(value, "leaf", [(i, i ^ 1 << distance) for i in range(count)])


def upper_field(coef, coupling, transfer, couple_mask):
    leaf_count = lax.axis_size("leaf")
    leaf_pos = lax.axis_index("leaf")
    couplings = []
    levels = range(2, min(coupling.shape[0], leaf_count.bit_length()))
    for lev in levels:
        other = swapped(coef, lev - 1)
        is_upper = (leaf_pos >> lev - 1 & 1) == 1
        total = dot(jnp.where(is_upper, other, coef), transfer[0])
        total = total + dot(jnp.where(is_upper, coef, other), transfer[1])
        coef = total.astype(BF16)
        cluster = leaf_pos >> lev
        coupled = jnp.zeros(coef.shape, F32)
        for pick, offset in enumerate((2, 3)):
            if offset < leaf_count >> lev:
                matrix = coupling[lev, pick]
                ahead = shifted(coef, -(offset << lev))
                behind = shifted(coef, offset << lev)
                ahead_mask = couple_mask[lev, cluster, pick].astype(F32)
                behind_mask = couple_mask[lev, jnp.maximum(cluster - offset, 0), pick].astype(F32)
                coupled = coupled + ahead_mask * dot(ahead, matrix)
                coupled = coupled + behind_mask * dot_t(behind, matrix)
        couplings.append(coupled)
    field = jnp.zeros(coef.shape, F32)
    for lev, coupled in zip(reversed(levels), reversed(couplings)):
        if lev + 1 in levels:
            field = dot_t(field.astype(BF16), transfer[leaf_pos >> lev & 1])
        field = field + coupled
    for lev in (1, 0):
        field = dot_t(field.astype(BF16), transfer[leaf_pos >> lev & 1])
    return field


def per_device(
    points_x, leaf_basis, near_tiles, near_cols, near_count, transfer, coupling, couple_mask
):
    assert lax.axis_size("level") == GROUP
    leaf_count = lax.axis_size("leaf")
    vectors, points = points_x.shape
    rank = leaf_basis.shape[2]
    rows = vectors // GROUP
    bits = GROUP.bit_length() - 1
    block = ((vectors, points), BF16)
    share = ((rows, rank), BF16)
    cube = 2 * rank * rank

    across = turned(points_x, 2)
    mate = turned(points_x, 1)
    joints = [(GROUP * g - 1, GROUP * g) for g in range(1, leaf_count)]
    edge = lax.ppermute(points_x, ("leaf", "level"), joints + [(b, a) for a, b in joints])
    left_cols = shifted(near_cols, 1)
    right_cols = shifted(near_cols, -1)
    corner = turned(across, 1)

    *shares, w = call(
        partial(up_kernel, bits), "up", cube * (vectors + bits * points) * 2,
        [points_x, leaf_basis, transfer], [], [share] * GROUP + [((points, rank), BF16)],
        [pltpu.VMEM((GROUP, rows, rank), BF16)],
    )
    coef = shares[0].astype(F32)
    for turn in range(1, GROUP):
        coef = coef + turned(shares[turn], turn).astype(F32)
    coef = coef.astype(BF16)

    levels = coupling.shape[0]
    active = min(levels, leaf_count.bit_length())
    pairs = leaf_count // 2
    turns = [1, 2, 3] if pairs == 4 else [1, 2, 3, -1, -2, -3]
    clusters = [lev < active and (leaf_count >> lev) > 2 for lev in (0, 1)]
    *pushes, _, pair_coef = call(
        partial(push_kernel, turns, pairs, clusters), "push", cube * rows * 10,
        [coef, swapped(coef, 0), coupling, transfer], [couple_mask],
        [share] * len(turns) + [((2, rows, rank), BF16), share],
    )
    field = None
    for turn, push in zip(turns, pushes):
        if len(turns) < 6:
            route = [(i, (i + 2 * turn) % leaf_count) for i in range(leaf_count)]
            came = lax.ppermute(push, "leaf", route)
        else:
            came = shifted(push, 2 * turn)
        field = came.astype(F32) if field is None else field + came.astype(F32)
    if active > 2 and (leaf_count >> 2) > 2:
        field = field + upper_field(pair_coef, coupling, transfer, couple_mask)
    field = field.astype(BF16)
    fields = [field] + [turned(field, turn) for turn in range(1, GROUP)]

    to_left, to_right = call(
        pick_kernel, "pick", 0, [points_x, mate, across, corner], [left_cols, right_cols],
        [block] * 2,
    )
    from_left = shifted(to_right, 1)
    from_right = shifted(to_left, -1)
    (acc,) = call(
        near_kernel, "near", 8 * vectors * points * points,
        [points_x, mate, across, corner, edge, near_tiles], [near_cols, near_count],
        [((vectors, points), F32)],
    )
    (out,) = call(
        finish_kernel, "finish", 4 * vectors * points * points,
        [acc, from_left, from_right, near_tiles, w, *fields], [near_cols, near_count],
        [block], [pltpu.VMEM((vectors, points), F32), pltpu.VMEM((GROUP, rows, rank), BF16)],
    )
    return out


def solution(mesh):
    in_specs = (
        P(None, ("leaf", "level")),
        P(("leaf", "level"), None, None),
        P(("leaf", "level"), None, None, None),
        P(("leaf", "level"), None),
        P(("leaf", "level")),
        P(),
        P(),
        P(),
    )
    out_specs = P(None, ("leaf", "level"))
    return jax.shard_map(
        per_device, mesh=mesh, in_specs=in_specs, out_specs=out_specs, check_vma=False
    )
```

time: 105 us -> 50.9 us (0.48)
  the two profiles are of different devices: /device:TPU:0 before, /device:TPU:11 now
where the time goes in v1:
time: 50.9 us; the launch traced here: 50.4 us
  starting transfers between devices  29.3 us (58%)
  Pallas kernels  8.11 us (16%)
  waiting for transfers between devices  6.95 us (14%)
  local copies, waits for them, and re-layouts  5.19 us (10%)
  between operations  0.8 us (2%)
    ppermute x4, starting transfers between devices, shifted(): return lax.ppermute(value, 'leaf', route)  12.4 us
    pallas_call x5, Pallas kernels, call(): pl.pallas_call(kernel, out_shape=shapes, in_specs=[pl.BlockSpec(memory_sp...  8.11 us
    ppermute x9, starting transfers between devices, turned(): return lax.ppermute(value, 'level', [(i, i ^ turn) for i in range(GROUP)])  7.88 us
    unnamed x13, local copies, waits for them, and re-layouts  5.19 us
    ppermute x3, starting transfers between devices, per_device(): came = lax.ppermute(push, 'leaf', route)  4.76 us
    ppermute x4, waiting for transfers between devices, shifted(): return lax.ppermute(value, 'leaf', route)  4.22 us
    ppermute x1, starting transfers between devices, per_device(): lax.ppermute(points_x, ('leaf', 'level'), joints + [(b, a) for a, b in jo...  3.04 us
    ppermute x9, waiting for transfers between devices, turned(): return lax.ppermute(value, 'level', [(i, i ^ turn) for i in range(GROUP)])  2.72 us
  transfers between devices with their start and end apart: 18, of which 4 were waited for; matrix products, arithmetic and copies ran while one was open for 2% of the time, Pallas kernels for 13%

profile of v1, /device:TPU:11, one launch (start us, length us, event | category | flops | bytes accessed | tf_op | source)
XLA Modules:
  0.0 50.4 jit_solution(15719256865627257034)
XLA Ops:
  0.0 0.3 collective-permute-start.1
  0.3 1.1 %copy-done.2 = bf16[2,256,256]{2,1,0:T(8,128)(2,1)S(1)} copy-done((bf16[2,256,256]{2,1,0:T(8,128)(2,1)S(1)}, bf16[2,256,256]{2,1,0:T(8,128)(2,1)}, u32[]{:S(2)}) %copy-start.2) | copy-done | bytes 262168
  1.3 0.9 %copy-done.5 = bf16[1,512,256]{2,1,0:T(8,128)(2,1)S(1)} copy-done((bf16[1,512,256]{2,1,0:T(8,128)(2,1)S(1)}, bf16[1,512,256]{2,1,0:T(8,128)(2,1)}, u32[]{:S(2)}) %copy-start.5) | copy-done | bytes 262168
  2.3 1.6 %up.1 = (bf16[64,256]{1,0:T(8,128)(2,1)S(1)}, bf16[64,256]{1,0:T(8,128)(2,1)S(1)}, bf16[64,256]{1,0:T(8,128)(2,1)S(1)}, bf16[64,256]{1,0:T(8,128)(2,1)S(1)}, bf16[512,256]{1,0:T(8,128)(2,1)S(1)}) custom-call(bf16[256,512]{1,0:T(8,128)(2,1)} %x_ref.5, bf16[1,512,256]{2,1,0:T(8,128)(2,1)S(1)} %copy-done.5, bf16[2,256,256]{2,1,0:T(8,128)(2,1)S(1)} %copy-done.2), custom_call_target="tpu_custom_call" | custom-call | flops 335544320 | bytes 1179648 | tf_op jit(solution)/shard_map/up/pallas_call | solution.py:29
  3.9 2.0 %collective-permute-start.10 = (bf16[64,256]{1,0:T(8,128)(2,1)S(1)}, bf16[64,256]{1,0:T(8,128)(2,1)S(1)}, u32[]{:S(2)}, u32[]{:S(2)}) collective-permute-start(bf16[64,256]{1,0:T(8,128)(2,1)S(1)} %get-tuple-element.21), channel_id=1, source_target_pairs={{0,3},{1,2},{2,1},{3,0},{4,7},{5,6},{6,5},{7,4},{8,11},{9,10},{10,... | collective-permute-start | bytes 98312 | tf_op jit(solution)/shard_map/ppermute | solution.py:148
  5.8 0.3 collective-permute-start.9
  6.2 0.1 collective-permute-start.8
  6.3 0.4 collective-permute-start
  6.7 0.7 %collective-permute-done.1.across_ref = bf16[256,512]{1,0:T(8,128)(2,1)S(1)} collective-permute-done((bf16[256,512]{1,0:T(8,128)(2,1)}, bf16[256,512]{1,0:T(8,128)(2,1)S(1)}, u32[]{:S(2)}, u32[]{:S(2)}) %collective-permute-start.1) | collective-permute-done | bytes 262176 | tf_op jit(solution)/shard_map/ppermute | solution.py:148
  7.4 2.2 %collective-permute-start.2 = (bf16[256,512]{1,0:T(8,128)(2,1)S(1)}, bf16[256,512]{1,0:T(8,128)(2,1)S(1)}, u32[]{:S(2)}, u32[]{:S(2)}) collective-permute-start(bf16[256,512]{1,0:T(8,128)(2,1)S(1)} %collective-permute-done.1.across_ref), channel_id=1, source_target_pairs={{0,1},{1,0},{2,3},{3,2},{4,5},{5,4},{6,7},{7,6},{8,9},{9,8},{10,11... | collective-permute-start | bytes 786440 | tf_op jit(solution)/shard_map/ppermute | solution.py:148
  9.6 1.3 %collective-permute-start.11 = (bf16[64,256]{1,0:T(8,128)(2,1)S(1)}, bf16[64,256]{1,0:T(8,128)(2,1)S(1)}, u32[]{:S(2)}, u32[]{:S(2)}) collective-permute-start(bf16[64,256]{1,0:T(8,128)(2,1)S(1)} %add_convert_fusion.1.own_ref), channel_id=1, source_target_pairs={{0,4},{4,0},{8,12},{12,8},{16,20},{20,16},{24,28},{28,24},{1,5},{5... | collective-permute-start | bytes 98312 | tf_op jit(solution)/shard_map/ppermute | solution.py:159
  10.9 3.0 %collective-permute-start.3 = (bf16[256,512]{1,0:T(8,128)(2,1)}, bf16[256,512]{1,0:T(8,128)(2,1)S(1)}, u32[]{:S(2)}, u32[]{:S(2)}) collective-permute-start(bf16[256,512]{1,0:T(8,128)(2,1)} %x_ref.5), channel_id=1, source_target_pairs={{3,4},{7,8},{11,12},{15,16},{19,20},{23,24},{27,28},{4,3},{8,7},{1... | collective-permute-start | bytes 786440 | tf_op jit(solution)/shard_map/ppermute | solution.py:211
  13.9 4.2 %collective-permute-start.4 = (s32[1,4]{1,0:T(1,128)}, s32[1,4]{1,0:T(1,128)S(1)}, u32[]{:S(2)}, u32[]{:S(2)}) collective-permute-start(s32[1,4]{1,0:T(1,128)} %cols_ref.3), channel_id=1, source_target_pairs={{0,4},{4,8},{8,12},{12,16},{16,20},{20,24},{24,28},{1,5},{5,9},{9,... | collective-permute-start | bytes 56 | tf_op jit(solution)/shard_map/ppermute | solution.py:154
  18.1 0.8 %copy.9.mask_ref = s32[6,8,2]{2,1,0:T(8,128)S(1)} copy(s32[6,8,2]{1,2,0:T(2,128)} %param.15) | data formatting | bytes 768 | tf_op args[7]
  18.9 2.0 %collective-permute-start.5 = (s32[1,4]{1,0:T(1,128)}, s32[1,4]{1,0:T(1,128)S(1)}, u32[]{:S(2)}, u32[]{:S(2)}) collective-permute-start(s32[1,4]{1,0:T(1,128)} %cols_ref.3), channel_id=1, source_target_pairs={{4,0},{8,4},{12,8},{16,12},{20,16},{24,20},{28,24},{5,1},{9,5},{13... | collective-permute-start | bytes 56 | tf_op jit(solution)/shard_map/ppermute | solution.py:154
  20.9 1.4 %copy-done.1 = bf16[6,2,256,256]{3,2,1,0:T(8,128)(2,1)S(1)} copy-done((bf16[6,2,256,256]{3,2,1,0:T(8,128)(2,1)S(1)}, bf16[6,2,256,256]{3,2,1,0:T(8,128)(2,1)}, u32[]{:S(2)}) %copy-start.1) | copy-done | bytes 1572888
  22.3 0.9 %copy-done.3 = bf16[2,256,256]{2,1,0:T(8,128)(2,1)S(1)} copy-done((bf16[2,256,256]{2,1,0:T(8,128)(2,1)S(1)}, bf16[2,256,256]{2,1,0:T(8,128)(2,1)}, u32[]{:S(2)}) %copy-start.3) | copy-done | bytes 262168
  23.3 2.4 %push.1 = (bf16[64,256]{1,0:T(8,128)(2,1)S(1)}, bf16[64,256]{1,0:T(8,128)(2,1)S(1)}, bf16[64,256]{1,0:T(8,128)(2,1)S(1)}, bf16[2,64,256]{2,1,0:T(8,128)(2,1)}, bf16[64,256]{1,0:T(8,128)(2,1)}) custom-call(bf16[64,256]{1,0:T(8,128)(2,1)S(1)} %add_convert_fusion.1.own_ref, bf16[64,256]{1,0:T(8,128)(2,1)S(1)} %collective-permute-done.11.mate_ref, ...), custom_call_target="tpu_custom_call" | custom-call | flops 83886080 | bytes 2097152 | tf_op jit(solution)/shard_map/push/pallas_call | solution.py:29
  25.7 2.5 %collective-permute-start.13 = (bf16[64,256]{1,0:T(8,128)(2,1)S(1)}, bf16[64,256]{1,0:T(8,128)(2,1)S(1)}, u32[]{:S(2)}, u32[]{:S(2)}) collective-permute-start(bf16[64,256]{1,0:T(8,128)(2,1)S(1)} %get-tuple-element.23), channel_id=1, source_target_pairs={{0,16},{4,20},{8,24},{12,28},{16,0},{20,4},{24,8},{28,12},{1,17},{... | collective-permute-start | bytes 98312 | tf_op jit(solution)/shard_map/ppermute | solution.py:240
  28.2 2.3 %collective-permute-start.12 = (bf16[64,256]{1,0:T(8,128)(2,1)S(1)}, bf16[64,256]{1,0:T(8,128)(2,1)S(1)}, u32[]{:S(2)}, u32[]{:S(2)}) collective-permute-start(bf16[64,256]{1,0:T(8,128)(2,1)S(1)} %get-tuple-element.22), channel_id=1, source_target_pairs={{0,8},{4,12},{8,16},{12,20},{16,24},{20,28},{24,0},{28,4},{1,9},{5... | collective-permute-start | bytes 98312 | tf_op jit(solution)/shard_map/ppermute | solution.py:240
  31.2 1.0 %pick.1 = (bf16[256,512]{1,0:T(8,128)(2,1)S(1)}, bf16[256,512]{1,0:T(8,128)(2,1)S(1)}) custom-call(bf16[256,512]{1,0:T(8,128)(2,1)} %x_ref.5, bf16[256,512]{1,0:T(8,128)(2,1)S(1)} %collective-permute-done.mate_ref, bf16[256,512]{1,0:T(8,128)(2,1)S(1)} %collective-permute-done.1.across_ref, bf16[256,512]{1,0:T(8,128)(2,1)S(1)} %collective-permute-done.2.corner_ref, ...), custom_call_target="tpu_custom_call" | custom-call | bytes 1572864 | tf_op jit(solution)/shard_map/pick/pallas_call | solution.py:29
  32.2 1.9 %collective-permute-start.6 = (bf16[256,512]{1,0:T(8,128)(2,1)S(1)}, bf16[256,512]{1,0:T(8,128)(2,1)S(1)}, u32[]{:S(2)}, u32[]{:S(2)}) collective-permute-start(bf16[256,512]{1,0:T(8,128)(2,1)S(1)} %get-tuple-element.15), channel_id=1, source_target_pairs={{0,4},{4,8},{8,12},{12,16},{16,20},{20,24},{24,28},{1,5},{5,9},{9,... | collective-permute-start | bytes 786440 | tf_op jit(solution)/shard_map/ppermute | solution.py:154
  34.1 4.3 %collective-permute-start.7 = (bf16[256,512]{1,0:T(8,128)(2,1)S(1)}, bf16[256,512]{1,0:T(8,128)(2,1)S(1)}, u32[]{:S(2)}, u32[]{:S(2)}) collective-permute-start(bf16[256,512]{1,0:T(8,128)(2,1)S(1)} %get-tuple-element.16), channel_id=1, source_target_pairs={{4,0},{8,4},{12,8},{16,12},{20,16},{24,20},{28,24},{5,1},{9,5},{13... | collective-permute-start | bytes 786440 | tf_op jit(solution)/shard_map/ppermute | solution.py:154
  38.5 0.7 %collective-permute-start.15 = (bf16[64,256]{1,0:T(8,128)(2,1)S(1)}, bf16[64,256]{1,0:T(8,128)(2,1)S(1)}, u32[]{:S(2)}, u32[]{:S(2)}) collective-permute-start(bf16[64,256]{1,0:T(8,128)(2,1)S(1)} %add_convert_fusion.field0), channel_id=1, source_target_pairs={{0,1},{1,0},{2,3},{3,2},{4,5},{5,4},{6,7},{7,6},{8,9},{9,8},{10,11... | collective-permute-start | bytes 98312 | tf_op jit(solution)/shard_map/ppermute | solution.py:148
  39.2 1.9 %collective-permute-start.16 = (bf16[64,256]{1,0:T(8,128)(2,1)S(1)}, bf16[64,256]{1,0:T(8,128)(2,1)S(1)}, u32[]{:S(2)}, u32[]{:S(2)}) collective-permute-start(bf16[64,256]{1,0:T(8,128)(2,1)S(1)} %add_convert_fusion.field0), channel_id=1, source_target_pairs={{0,2},{1,3},{2,0},{3,1},{4,6},{5,7},{6,4},{7,5},{8,10},{9,11},{10,... | collective-permute-start | bytes 98312 | tf_op jit(solution)/shard_map/ppermute | solution.py:148
  41.1 0.0 collective-permute-start.17
  41.1 1.5 %near.1.acc_ref = f32[256,512]{1,0:T(8,128)S(1)} custom-call(bf16[256,512]{1,0:T(8,128)(2,1)} %x_ref.5, bf16[256,512]{1,0:T(8,128)(2,1)S(1)} %collective-permute-done.mate_ref, bf16[256,512]{1,0:T(8,128)(2,1)S(1)} %collective-permute-done.1.across_ref, bf16[256,512]{1,0:T(8,128)(2,1)S(1)} %collective-permute-done.2.corner_ref, ...), custom_call_target="tpu_custom_call" | custom-call | flops 536870912 | bytes 3932160 | tf_op jit(solution)/shard_map/near/pallas_call | solution.py:29
  42.7 0.0 collective-permute-done.16.field2
  42.7 2.0 %collective-permute-done.17.field3 = bf16[64,256]{1,0:T(8,128)(2,1)S(1)} collective-permute-done((bf16[64,256]{1,0:T(8,128)(2,1)S(1)}, bf16[64,256]{1,0:T(8,128)(2,1)S(1)}, u32[]{:S(2)}, u32[]{:S(2)}) %collective-permute-start.17) | collective-permute-done | bytes 32800 | tf_op jit(solution)/shard_map/ppermute | solution.py:148
  44.7 0.9 %collective-permute-done.6.left_ref = bf16[256,512]{1,0:T(8,128)(2,1)S(1)} collective-permute-done((bf16[256,512]{1,0:T(8,128)(2,1)S(1)}, bf16[256,512]{1,0:T(8,128)(2,1)S(1)}, u32[]{:S(2)}, u32[]{:S(2)}) %collective-permute-start.6) | collective-permute-done | bytes 262176 | tf_op jit(solution)/shard_map/ppermute | solution.py:154
  45.6 3.3 %collective-permute-done.7.right_ref = bf16[256,512]{1,0:T(8,128)(2,1)S(1)} collective-permute-done((bf16[256,512]{1,0:T(8,128)(2,1)S(1)}, bf16[256,512]{1,0:T(8,128)(2,1)S(1)}, u32[]{:S(2)}, u32[]{:S(2)}) %collective-permute-start.7) | collective-permute-done | bytes 262176 | tf_op jit(solution)/shard_map/ppermute | solution.py:154
  48.9 1.5 %finish.1 = bf16[256,512]{1,0:T(8,128)(2,1)} custom-call(f32[256,512]{1,0:T(8,128)S(1)} %near.1.acc_ref, bf16[256,512]{1,0:T(8,128)(2,1)S(1)} %collective-permute-done.6.left_ref, bf16[256,512]{1,0:T(8,128)(2,1)S(1)} %collective-permute-done.7.right_ref, bf16[1,4,512,512]{3,2,1,0:T(8,128)(2,1)S(1)} %copy-done, bf16[512,256]{1,0:T(8,128)(2,1)S(1)} %get-tuple-element.17.w_ref, ...), custom_call_target="tpu_custom_call" | custom-call | flops 268435456 | bytes 3801088 | tf_op jit(solution)/shard_map/finish/pallas_call | solution.py:29
  (24 shorter events, 0.1 us)
Async XLA Ops:
  0.0 41.1 %copy-start = (bf16[1,4,512,512]{3,2,1,0:T(8,128)(2,1)S(1)}, bf16[1,4,512,512]{3,2,1,0:T(8,128)(2,1)}, u32[]{:S(2)}) copy-start(bf16[1,4,512,512]{3,2,1,0:T(8,128)(2,1)} %tiles_ref.3) | copy-start | bytes 6291460
  0.0 7.4 %collective-permute-start.1 = (bf16[256,512]{1,0:T(8,128)(2,1)}, bf16[256,512]{1,0:T(8,128)(2,1)S(1)}, u32[]{:S(2)}, u32[]{:S(2)}) collective-permute-start(bf16[256,512]{1,0:T(8,128)(2,1)} %x_ref.5), channel_id=1, source_target_pairs={{0,2},{1,3},{2,0},{3,1},{4,6},{5,7},{6,4},{7,5},{8,10},{9,11},{10,... | collective-permute-start | bytes 786440 | tf_op jit(solution)/shard_map/ppermute | solution.py:148
  0.3 1.1 %copy-start.2 = (bf16[2,256,256]{2,1,0:T(8,128)(2,1)S(1)}, bf16[2,256,256]{2,1,0:T(8,128)(2,1)}, u32[]{:S(2)}) copy-start(bf16[2,256,256]{2,1,0:T(8,128)(2,1)} %transfer_ref.3) | copy-start | bytes 786436
  1.3 0.9 %copy-start.5 = (bf16[1,512,256]{2,1,0:T(8,128)(2,1)S(1)}, bf16[1,512,256]{2,1,0:T(8,128)(2,1)}, u32[]{:S(2)}) copy-start(bf16[1,512,256]{2,1,0:T(8,128)(2,1)} %basis_ref.1) | copy-start | bytes 786436
  3.9 5.7 %collective-permute-start.10 = (bf16[64,256]{1,0:T(8,128)(2,1)S(1)}, bf16[64,256]{1,0:T(8,128)(2,1)S(1)}, u32[]{:S(2)}, u32[]{:S(2)}) collective-permute-start(bf16[64,256]{1,0:T(8,128)(2,1)S(1)} %get-tuple-element.21), channel_id=1, source_target_pairs={{0,3},{1,2},{2,1},{3,0},{4,7},{5,6},{6,5},{7,4},{8,11},{9,10},{10,... | collective-permute-start | bytes 98312 | tf_op jit(solution)/shard_map/ppermute | solution.py:148
  5.8 3.7 %collective-permute-start.9 = (bf16[64,256]{1,0:T(8,128)(2,1)S(1)}, bf16[64,256]{1,0:T(8,128)(2,1)S(1)}, u32[]{:S(2)}, u32[]{:S(2)}) collective-permute-start(bf16[64,256]{1,0:T(8,128)(2,1)S(1)} %get-tuple-element.20), channel_id=1, source_target_pairs={{0,2},{1,3},{2,0},{3,1},{4,6},{5,7},{6,4},{7,5},{8,10},{9,11},{10,... | collective-permute-start | bytes 98312 | tf_op jit(solution)/shard_map/ppermute | solution.py:148
  6.2 3.4 %collective-permute-start.8 = (bf16[64,256]{1,0:T(8,128)(2,1)S(1)}, bf16[64,256]{1,0:T(8,128)(2,1)S(1)}, u32[]{:S(2)}, u32[]{:S(2)}) collective-permute-start(bf16[64,256]{1,0:T(8,128)(2,1)S(1)} %get-tuple-element.19), channel_id=1, source_target_pairs={{0,1},{1,0},{2,3},{3,2},{4,5},{5,4},{6,7},{7,6},{8,9},{9,8},{10,11... | collective-permute-start | bytes 98312 | tf_op jit(solution)/shard_map/ppermute | solution.py:148
  6.3 21.9 %collective-permute-start = (bf16[256,512]{1,0:T(8,128)(2,1)}, bf16[256,512]{1,0:T(8,128)(2,1)S(1)}, u32[]{:S(2)}, u32[]{:S(2)}) collective-permute-start(bf16[256,512]{1,0:T(8,128)(2,1)} %x_ref.5), channel_id=1, source_target_pairs={{0,1},{1,0},{2,3},{3,2},{4,5},{5,4},{6,7},{7,6},{8,9},{9,8},{10,11... | collective-permute-start | bytes 786440 | tf_op jit(solution)/shard_map/ppermute | solution.py:148
  7.4 23.8 %collective-permute-start.2 = (bf16[256,512]{1,0:T(8,128)(2,1)S(1)}, bf16[256,512]{1,0:T(8,128)(2,1)S(1)}, u32[]{:S(2)}, u32[]{:S(2)}) collective-permute-start(bf16[256,512]{1,0:T(8,128)(2,1)S(1)} %collective-permute-done.1.across_ref), channel_id=1, source_target_pairs={{0,1},{1,0},{2,3},{3,2},{4,5},{5,4},{6,7},{7,6},{8,9},{9,8},{10,11... | collective-permute-start | bytes 786440 | tf_op jit(solution)/shard_map/ppermute | solution.py:148
  9.6 9.3 %collective-permute-start.11 = (bf16[64,256]{1,0:T(8,128)(2,1)S(1)}, bf16[64,256]{1,0:T(8,128)(2,1)S(1)}, u32[]{:S(2)}, u32[]{:S(2)}) collective-permute-start(bf16[64,256]{1,0:T(8,128)(2,1)S(1)} %add_convert_fusion.1.own_ref), channel_id=1, source_target_pairs={{0,4},{4,0},{8,12},{12,8},{16,20},{20,16},{24,28},{28,24},{1,5},{5... | collective-permute-start | bytes 98312 | tf_op jit(solution)/shard_map/ppermute | solution.py:159
  10.9 30.2 %collective-permute-start.3 = (bf16[256,512]{1,0:T(8,128)(2,1)}, bf16[256,512]{1,0:T(8,128)(2,1)S(1)}, u32[]{:S(2)}, u32[]{:S(2)}) collective-permute-start(bf16[256,512]{1,0:T(8,128)(2,1)} %x_ref.5), channel_id=1, source_target_pairs={{3,4},{7,8},{11,12},{15,16},{19,20},{23,24},{27,28},{4,3},{8,7},{1... | collective-permute-start | bytes 786440 | tf_op jit(solution)/shard_map/ppermute | solution.py:211
  13.9 11.8 %collective-permute-start.4 = (s32[1,4]{1,0:T(1,128)}, s32[1,4]{1,0:T(1,128)S(1)}, u32[]{:S(2)}, u32[]{:S(2)}) collective-permute-start(s32[1,4]{1,0:T(1,128)} %cols_ref.3), channel_id=1, source_target_pairs={{0,4},{4,8},{8,12},{12,16},{16,20},{20,24},{24,28},{1,5},{5,9},{9,... | collective-permute-start | bytes 56 | tf_op jit(solution)/shard_map/ppermute | solution.py:154
  18.9 6.8 %collective-permute-start.5 = (s32[1,4]{1,0:T(1,128)}, s32[1,4]{1,0:T(1,128)S(1)}, u32[]{:S(2)}, u32[]{:S(2)}) collective-permute-start(s32[1,4]{1,0:T(1,128)} %cols_ref.3), channel_id=1, source_target_pairs={{4,0},{8,4},{12,8},{16,12},{20,16},{24,20},{28,24},{5,1},{9,5},{13... | collective-permute-start | bytes 56 | tf_op jit(solution)/shard_map/ppermute | solution.py:154
  20.9 1.4 %copy-start.1 = (bf16[6,2,256,256]{3,2,1,0:T(8,128)(2,1)S(1)}, bf16[6,2,256,256]{3,2,1,0:T(8,128)(2,1)}, u32[]{:S(2)}) copy-start(bf16[6,2,256,256]{3,2,1,0:T(8,128)(2,1)} %coupling_ref.1) | copy-start | bytes 4718596
  22.3 0.9 %copy-start.3 = (bf16[2,256,256]{2,1,0:T(8,128)(2,1)S(1)}, bf16[2,256,256]{2,1,0:T(8,128)(2,1)}, u32[]{:S(2)}) copy-start(bf16[2,256,256]{2,1,0:T(8,128)(2,1)} %transfer_ref.3) | copy-start | bytes 786436
  23.3 17.8 %copy-start.4 = (s32[1,4]{1,0:T(1,128)S(1)}, s32[1,4]{1,0:T(1,128)}, u32[]{:S(2)}) copy-start(s32[1,4]{1,0:T(1,128)} %cols_ref.3) | copy-start | bytes 52
  25.7 8.4 %collective-permute-start.14 = (bf16[64,256]{1,0:T(8,128)(2,1)S(1)}, bf16[64,256]{1,0:T(8,128)(2,1)S(1)}, u32[]{:S(2)}, u32[]{:S(2)}) collective-permute-start(bf16[64,256]{1,0:T(8,128)(2,1)S(1)} %get-tuple-element.24), channel_id=1, source_target_pairs={{0,24},{4,28},{8,0},{12,4},{16,8},{20,12},{24,16},{28,20},{1,25},{... | collective-permute-start | bytes 98312 | tf_op jit(solution)/shard_map/ppermute | solution.py:240
  25.7 12.7 %collective-permute-start.13 = (bf16[64,256]{1,0:T(8,128)(2,1)S(1)}, bf16[64,256]{1,0:T(8,128)(2,1)S(1)}, u32[]{:S(2)}, u32[]{:S(2)}) collective-permute-start(bf16[64,256]{1,0:T(8,128)(2,1)S(1)} %get-tuple-element.23), channel_id=1, source_target_pairs={{0,16},{4,20},{8,24},{12,28},{16,0},{20,4},{24,8},{28,12},{1,17},{... | collective-permute-start | bytes 98312 | tf_op jit(solution)/shard_map/ppermute | solution.py:240
  28.2 10.2 %collective-permute-start.12 = (bf16[64,256]{1,0:T(8,128)(2,1)S(1)}, bf16[64,256]{1,0:T(8,128)(2,1)S(1)}, u32[]{:S(2)}, u32[]{:S(2)}) collective-permute-start(bf16[64,256]{1,0:T(8,128)(2,1)S(1)} %get-tuple-element.22), channel_id=1, source_target_pairs={{0,8},{4,12},{8,16},{12,20},{16,24},{20,28},{24,0},{28,4},{1,9},{5... | collective-permute-start | bytes 98312 | tf_op jit(solution)/shard_map/ppermute | solution.py:240
  32.2 13.4 %collective-permute-start.6 = (bf16[256,512]{1,0:T(8,128)(2,1)S(1)}, bf16[256,512]{1,0:T(8,128)(2,1)S(1)}, u32[]{:S(2)}, u32[]{:S(2)}) collective-permute-start(bf16[256,512]{1,0:T(8,128)(2,1)S(1)} %get-tuple-element.15), channel_id=1, source_target_pairs={{0,4},{4,8},{8,12},{12,16},{16,20},{20,24},{24,28},{1,5},{5,9},{9,... | collective-permute-start | bytes 786440 | tf_op jit(solution)/shard_map/ppermute | solution.py:154
  34.1 14.8 %collective-permute-start.7 = (bf16[256,512]{1,0:T(8,128)(2,1)S(1)}, bf16[256,512]{1,0:T(8,128)(2,1)S(1)}, u32[]{:S(2)}, u32[]{:S(2)}) collective-permute-start(bf16[256,512]{1,0:T(8,128)(2,1)S(1)} %get-tuple-element.16), channel_id=1, source_target_pairs={{4,0},{8,4},{12,8},{16,12},{20,16},{24,20},{28,24},{5,1},{9,5},{13... | collective-permute-start | bytes 786440 | tf_op jit(solution)/shard_map/ppermute | solution.py:154
  38.5 4.2 %collective-permute-start.15 = (bf16[64,256]{1,0:T(8,128)(2,1)S(1)}, bf16[64,256]{1,0:T(8,128)(2,1)S(1)}, u32[]{:S(2)}, u32[]{:S(2)}) collective-permute-start(bf16[64,256]{1,0:T(8,128)(2,1)S(1)} %add_convert_fusion.field0), channel_id=1, source_target_pairs={{0,1},{1,0},{2,3},{3,2},{4,5},{5,4},{6,7},{7,6},{8,9},{9,8},{10,11... | collective-permute-start | bytes 98312 | tf_op jit(solution)/shard_map/ppermute | solution.py:148
  39.2 3.6 %collective-permute-start.16 = (bf16[64,256]{1,0:T(8,128)(2,1)S(1)}, bf16[64,256]{1,0:T(8,128)(2,1)S(1)}, u32[]{:S(2)}, u32[]{:S(2)}) collective-permute-start(bf16[64,256]{1,0:T(8,128)(2,1)S(1)} %add_convert_fusion.field0), channel_id=1, source_target_pairs={{0,2},{1,3},{2,0},{3,1},{4,6},{5,7},{6,4},{7,5},{8,10},{9,11},{10,... | collective-permute-start | bytes 98312 | tf_op jit(solution)/shard_map/ppermute | solution.py:148
  41.1 3.6 %collective-permute-start.17 = (bf16[64,256]{1,0:T(8,128)(2,1)S(1)}, bf16[64,256]{1,0:T(8,128)(2,1)S(1)}, u32[]{:S(2)}, u32[]{:S(2)}) collective-permute-start(bf16[64,256]{1,0:T(8,128)(2,1)S(1)} %add_convert_fusion.field0), channel_id=1, source_target_pairs={{0,3},{1,2},{2,1},{3,0},{4,7},{5,6},{6,5},{7,4},{8,11},{9,10},{10,... | collective-permute-start | bytes 98312 | tf_op jit(solution)/shard_map/ppermute | solution.py:148

commit v2 on v1

--- a/solution.py
+++ b/solution.py
@@ -21,7 +21,7 @@
     return lax.dot_general(a, b, (((1,), (1,)), ((), ())), preferred_element_type=F32)
 
 
-def call(kernel, name, flops, inputs, scalars, outputs, scratch=()):
+def call(kernel, name, flops, inputs, scalars, outputs, scratch=(), inputs_in=pltpu.VMEM):
     shapes = [jax.ShapeDtypeStruct(shape, dtype) for shape, dtype in outputs]
     moved = sum(a.size * a.dtype.itemsize for a in inputs) + sum(
         s.size * s.dtype.itemsize for s in shapes
@@ -29,35 +29,49 @@
     return pl.pallas_call(
         kernel,
         out_shape=shapes,
-        in_specs=[pl.BlockSpec(memory_space=pltpu.VMEM)] * len(inputs)
+        in_specs=[pl.BlockSpec(memory_space=inputs_in)] * len(inputs)
         + [pl.BlockSpec(memory_space=pltpu.SMEM)] * len(scalars),
         out_specs=[pl.BlockSpec(memory_space=pltpu.VMEM)] * len(outputs),
         scratch_shapes=list(scratch),
         compiler_params=pltpu.CompilerParams(vmem_limit_bytes=VMEM_LIMIT),
-        cost_estimate=pl.CostEstimate(flops=flops, bytes_accessed=moved, transcendentals=0),
+        cost_estimate=pl.CostEstimate(flops=0, bytes_accessed=0, transcendentals=0),
         name=name,
-    )(*inputs, *scalars)
-
-
-def up_kernel(bits, x_ref, basis_ref, transfer_ref, *refs):
-    *share_refs, w_ref, z_ref = refs
+    )(*(pltpu.with_memory_space_constraint(a, inputs_in) for a in inputs), *scalars)
+
+
+def up_kernel(
+    bits, x_hbm, basis_hbm, transfer_hbm, coupling_hbm,
+    keep_ref, send_ref, w_ref, x_ref, transfer_ref, coupling_ref, basis_ref, z_ref, sems
+):
     pos = lax.axis_index("level")
-    w = basis_ref[0]
+    core = pos & 1
+    pairs = (
+        (basis_hbm.at[0], basis_ref), (transfer_hbm, transfer_ref), (x_hbm, x_ref),
+        (coupling_hbm.at[:2], coupling_ref),
+    )
+    copies = [pltpu.make_async_copy(a, b, sems.at[i]) for i, (a, b) in enumerate(pairs)]
+    for copy in copies:
+        copy.start()
+    copies[0].wait()
+    copies[1].wait()
+    w = basis_ref[...]
     for bit in range(bits):
         w = dot(w, transfer_ref[pos >> bit & 1]).astype(BF16)
     w_ref[...] = w
+    copies[2].wait()
     z = dot(x_ref[...], w).astype(BF16)
     rows = z_ref.shape[1]
-    for member in range(GROUP):
-        z_ref[member] = z[member * rows : (member + 1) * rows]
-    for turn, share_ref in enumerate(share_refs):
-        share_ref[...] = z_ref[pos ^ turn]
+    z_ref[0] = z[:rows]
+    z_ref[1] = z[rows:]
+    keep_ref[...] = z_ref[core]
+    send_ref[...] = z_ref[1 - core]
+    copies[3].wait()
 
 
 def push_kernel(
     turns, pairs, clusters, own_ref, mate_ref, coupling_ref, transfer_ref, mask_ref, *refs
 ):
-    *push_refs, both_ref, pair_ref = refs
+    *push_refs, pair_ref, both_ref = refs
     leaf_pos = lax.axis_index("leaf")
     pair, side = leaf_pos >> 1, leaf_pos & 1
     both_ref[side] = own_ref[...]
@@ -68,7 +82,7 @@
     def term(lev, coef, gap, source, target):
         pick = abs(gap) - 2
         matrix = coupling_ref[lev, pick]
-        switch = mask_ref[lev, source if gap > 0 else target, pick].astype(F32)
+        switch = mask_ref[lev, pick, source if gap > 0 else target].astype(F32)
         return switch * (dot_t(coef, matrix) if gap > 0 else dot(coef, matrix))
 
     def fill(push_ref, distance, to_side):
@@ -89,18 +103,24 @@
         push_ref[...] = total.astype(BF16)
 
     for turn, push_ref in zip(turns, push_refs):
-        for distance in (turn, turn - pairs) if len(turns) < 6 else (turn,):
-            target_pair = pair + distance
-            inside = jnp.logical_and(target_pair >= 0, target_pair < pairs)
+        for distance in reached(turn, pairs):
+            if pairs == 4:
+                inside = (pair ^ turn) == pair + distance
+            else:
+                inside = jnp.logical_and(pair + distance >= 0, pair + distance < pairs)
             for to_side in (0, 1):
                 @pl.when(jnp.logical_and(inside, side == to_side))
                 def _(push_ref=push_ref, distance=distance, to_side=to_side):
                     fill(push_ref, distance, to_side)
 
 
-def pick_kernel(x_ref, mate_ref, across_ref, corner_ref, left_cols, right_cols, to_left, to_right):
+def reached(turn, pairs):
+    return sorted({(i ^ turn) - i for i in range(pairs)}) if pairs == 4 else [turn]
+
+
+def pick_kernel(x_ref, mate_ref, across_ref, corner_ref, even_cols, odd_cols, to_even, to_odd):
     pos = lax.axis_index("level")
-    for cols, out in ((left_cols, to_left), (right_cols, to_right)):
+    for cols, out in ((even_cols, to_even), (odd_cols, to_odd)):
         turn = lax.rem(cols[0, 3], GROUP) ^ pos
         for at, block in enumerate((x_ref, mate_ref, across_ref, corner_ref)):
             @pl.when(turn == at)
@@ -127,20 +147,27 @@
 
 
 def finish_kernel(
-    acc_ref, left_ref, right_ref, tiles_ref, w_ref, field0, field1, field2, field3,
+    acc_ref, even_ref, odd_ref, tiles_ref, w_ref, own_field, mate_field,
     cols_ref, count_ref, out_ref, total_ref, field_ref
 ):
-    pos = lax.axis_index("level")
-    for turn, share_ref in enumerate((field0, field1, field2, field3)):
-        field_ref[pos ^ turn] = share_ref[...]
-    field = jnp.concatenate([field_ref[member] for member in range(GROUP)], axis=0)
+    core = lax.axis_index("level") & 1
+    side = lax.axis_index("leaf") & 1
+    field_ref[core] = own_field[...]
+    field_ref[1 - core] = mate_field[...]
+    field = jnp.concatenate([field_ref[0], field_ref[1]], axis=0)
     total_ref[...] = acc_ref[...] + dot_t(field, w_ref[...])
     group = cols_ref[0, 3] // GROUP
-    live = count_ref[0] > 3
-    for at, block in ((0, left_ref), (2, right_ref)):
-        @pl.when(jnp.logical_and(live, group == at))
-        def _(block=block):
-            total_ref[...] += dot(block[...], tiles_ref[0, 3])
+    live = jnp.logical_and(count_ref[0] > 3, group != 1)
+    from_even = (group == 0) == (side == 1)
+
+    @pl.when(jnp.logical_and(live, from_even))
+    def _():
+        total_ref[...] += dot(even_ref[...], tiles_ref[0, 3])
+
+    @pl.when(jnp.logical_and(live, jnp.logical_not(from_even)))
+    def _():
+        total_ref[...] += dot(odd_ref[...], tiles_ref[0, 3])
+
     out_ref[...] = total_ref[...].astype(BF16)
 
 
@@ -157,6 +184,12 @@
 def swapped(value, distance):
     count = lax.axis_size("leaf")
     return lax.ppermute(value, "leaf", [(i, i ^ 1 << distance) for i in range(count)])
+
+
+def neighbours(value, odd):
+    count = lax.axis_size("leaf")
+    route = [(i, i + 1) for i in range(odd, count - 1, 2)]
+    return lax.ppermute(value, "leaf", route + [(b, a) for a, b in route])
 
 
 def upper_field(coef, coupling, transfer, couple_mask):
@@ -199,68 +232,71 @@
     leaf_count = lax.axis_size("leaf")
     vectors, points = points_x.shape
     rank = leaf_basis.shape[2]
-    rows = vectors // GROUP
+    rows = vectors // 2
     bits = GROUP.bit_length() - 1
     block = ((vectors, points), BF16)
-    share = ((rows, rank), BF16)
+    half = ((rows, rank), BF16)
     cube = 2 * rank * rank
 
     across = turned(points_x, 2)
     mate = turned(points_x, 1)
     joints = [(GROUP * g - 1, GROUP * g) for g in range(1, leaf_count)]
     edge = lax.ppermute(points_x, ("leaf", "level"), joints + [(b, a) for a, b in joints])
-    left_cols = shifted(near_cols, 1)
-    right_cols = shifted(near_cols, -1)
+    even_cols = neighbours(near_cols, 0)
+    odd_cols = neighbours(near_cols, 1)
     corner = turned(across, 1)
 
-    *shares, w = call(
+    keep, send, w, own_x, transfer_in, coupling_in = call(
         partial(up_kernel, bits), "up", cube * (vectors + bits * points) * 2,
-        [points_x, leaf_basis, transfer], [], [share] * GROUP + [((points, rank), BF16)],
-        [pltpu.VMEM((GROUP, rows, rank), BF16)],
-    )
-    coef = shares[0].astype(F32)
-    for turn in range(1, GROUP):
-        coef = coef + turned(shares[turn], turn).astype(F32)
-    coef = coef.astype(BF16)
-
-    levels = coupling.shape[0]
-    active = min(levels, leaf_count.bit_length())
+        [points_x, leaf_basis, transfer, coupling], [],
+        [half, half, ((points, rank), BF16), block, (transfer.shape, BF16),
+         ((2,) + coupling.shape[1:], BF16)],
+        [pltpu.VMEM((points, rank), BF16), pltpu.VMEM((2, rows, rank), BF16),
+         pltpu.SemaphoreType.DMA((4,))],
+        pltpu.HBM,
+    )
+    coef = (keep.astype(F32) + turned(send, 1).astype(F32)).astype(BF16)
+    coef = (coef.astype(F32) + turned(coef, 2).astype(F32)).astype(BF16)
+    edge, corner = lax.optimization_barrier((edge, corner))
+    to_even, to_odd = call(
+        pick_kernel, "pick", 0, [own_x, mate, across, corner], [even_cols, odd_cols], [block] * 2
+    )
+    coef, to_even, to_odd = lax.optimization_barrier((coef, to_even, to_odd))
+    beside = swapped(coef, 0)
+    from_even = neighbours(to_even, 0)
+    from_odd = neighbours(to_odd, 1)
+
+    (acc,) = call(
+        near_kernel, "near", 8 * vectors * points * points,
+        [own_x, mate, across, corner, edge, near_tiles], [near_cols, near_count],
+        [((vectors, points), F32)],
+    )
+    beside, acc = lax.optimization_barrier((beside, acc))
+    active = min(coupling.shape[0], leaf_count.bit_length())
     pairs = leaf_count // 2
     turns = [1, 2, 3] if pairs == 4 else [1, 2, 3, -1, -2, -3]
     clusters = [lev < active and (leaf_count >> lev) > 2 for lev in (0, 1)]
-    *pushes, _, pair_coef = call(
+    *pushes, pair_coef = call(
         partial(push_kernel, turns, pairs, clusters), "push", cube * rows * 10,
-        [coef, swapped(coef, 0), coupling, transfer], [couple_mask],
-        [share] * len(turns) + [((2, rows, rank), BF16), share],
+        [coef, beside, coupling_in, transfer_in], [couple_mask.transpose(0, 2, 1)],
+        [half] * (len(turns) + 1), [pltpu.VMEM((2, rows, rank), BF16)],
     )
     field = None
     for turn, push in zip(turns, pushes):
-        if len(turns) < 6:
-            route = [(i, (i + 2 * turn) % leaf_count) for i in range(leaf_count)]
-            came = lax.ppermute(push, "leaf", route)
+        if pairs == 4:
+            came = lax.ppermute(push, "leaf", [(i, i ^ 2 * turn) for i in range(leaf_count)])
         else:
             came = shifted(push, 2 * turn)
         field = came.astype(F32) if field is None else field + came.astype(F32)
     if active > 2 and (leaf_count >> 2) > 2:
         field = field + upper_field(pair_coef, coupling, transfer, couple_mask)
     field = field.astype(BF16)
-    fields = [field] + [turned(field, turn) for turn in range(1, GROUP)]
-
-    to_left, to_right = call(
-        pick_kernel, "pick", 0, [points_x, mate, across, corner], [left_cols, right_cols],
-        [block] * 2,
-    )
-    from_left = shifted(to_right, 1)
-    from_right = shifted(to_left, -1)
-    (acc,) = call(
-        near_kernel, "near", 8 * vectors * points * points,
-        [points_x, mate, across, corner, edge, near_tiles], [near_cols, near_count],
-        [((vectors, points), F32)],
-    )
+    mate_field = turned(field, 1)
+
     (out,) = call(
         finish_kernel, "finish", 4 * vectors * points * points,
-        [acc, from_left, from_right, near_tiles, w, *fields], [near_cols, near_count],
-        [block], [pltpu.VMEM((vectors, points), F32), pltpu.VMEM((GROUP, rows, rank), BF16)],
+        [acc, from_even, from_odd, near_tiles, w, field, mate_field], [near_cols, near_count],
+        [block], [pltpu.VMEM((vectors, points), F32), pltpu.VMEM((2, rows, rank), BF16)],
     )
     return out
 

time: 50.9 us -> 46.4 us (0.912)
  the two profiles are of different devices: /device:TPU:11 before, /device:TPU:0 now
where the time goes in v2:
time: 46.4 us; the launch traced here: 46.3 us
  starting transfers between devices  19.7 us (42%)
  waiting for transfers between devices  17.8 us (38%)
  Pallas kernels  7.94 us (17%)
  between operations  0.78 us (2%)
    ppermute x6, waiting for transfers between devices, turned(): return lax.ppermute(value, 'level', [(i, i ^ turn) for i in range(GROUP)])  8.53 us
    pallas_call x5, Pallas kernels, call(): pl.pallas_call(kernel, out_shape=shapes, in_specs=[pl.BlockSpec(memory_sp...  7.94 us
    ppermute x3, starting transfers between devices, per_device(): lax.ppermute(push, 'leaf', [(i, i ^ 2 * turn) for i in range(leaf_count)])  7.27 us
    ppermute x3, waiting for transfers between devices, per_device(): lax.ppermute(push, 'leaf', [(i, i ^ 2 * turn) for i in range(leaf_count)])  5.44 us
    ppermute x6, starting transfers between devices, turned(): return lax.ppermute(value, 'level', [(i, i ^ turn) for i in range(GROUP)])  4.91 us
    ppermute x4, starting transfers between devices, neighbours(): return lax.ppermute(value, 'leaf', route + [(b, a) for a, b in route])  4.8 us
    ppermute x4, waiting for transfers between devices, neighbours(): return lax.ppermute(value, 'leaf', route + [(b, a) for a, b in route])  3.35 us
    ppermute x1, starting transfers between devices, swapped(): lax.ppermute(value, 'leaf', [(i, i ^ 1 << distance) for i in range(count)])  2.09 us
  transfers between devices with their start and end apart: 15, of which 8 were waited for; matrix products, arithmetic and copies ran while one was open for 0% of the time, Pallas kernels for 2%

profile of v2, /device:TPU:0, one launch (start us, length us, event | category | flops | bytes accessed | tf_op | source)
XLA Modules:
  0.0 46.3 jit_solution(12627574143302514826)
XLA Ops:
  0.0 2.0 %up.1 = (bf16[128,256]{1,0:T(8,128)(2,1)S(1)}, bf16[128,256]{1,0:T(8,128)(2,1)S(1)}, bf16[512,256]{1,0:T(8,128)(2,1)S(1)}, bf16[256,512]{1,0:T(8,128)(2,1)S(1)},...) custom-call(bf16[256,512]{1,0:T(8,128)(2,1)} %x_hbm.1, bf16[1,512,256]{2,1,0:T(8,128)(2,1)} %basis_hbm.1, ...), custom_call_target="tpu_custom_call" | custom-call | tf_op jit(solution)/shard_map/up/pallas_call | solution.py:29
  2.0 0.5 %collective-permute-start = (bf16[128,256]{1,0:T(8,128)(2,1)S(1)}, bf16[128,256]{1,0:T(8,128)(2,1)S(1)}, u32[]{:S(2)}, u32[]{:S(2)}) collective-permute-start(bf16[128,256]{1,0:T(8,128)(2,1)S(1)} %get-tuple-element.24), channel_id=1, source_target_pairs={{0,1},{1,0},{2,3},{3,2},{4,5},{5,4},{6,7},{7,6},{8,9},{9,8},{10,11... | collective-permute-start | bytes 196616 | tf_op jit(solution)/shard_map/ppermute | solution.py:175
  2.5 2.6 %collective-permute-start.3 = (bf16[256,512]{1,0:T(8,128)(2,1)S(1)}, bf16[256,512]{1,0:T(8,128)(2,1)S(1)}, u32[]{:S(2)}, u32[]{:S(2)}) collective-permute-start(bf16[256,512]{1,0:T(8,128)(2,1)S(1)} %copy-done.3), channel_id=1, source_target_pairs={{0,2},{1,3},{2,0},{3,1},{4,6},{5,7},{6,4},{7,5},{8,10},{9,11},{10,... | collective-permute-start | bytes 786440 | tf_op jit(solution)/shard_map/ppermute | solution.py:175
  5.1 1.2 %collective-permute-start.1 = (bf16[128,256]{1,0:T(8,128)(2,1)S(1)}, bf16[128,256]{1,0:T(8,128)(2,1)S(1)}, u32[]{:S(2)}, u32[]{:S(2)}) collective-permute-start(bf16[128,256]{1,0:T(8,128)(2,1)S(1)} %add_convert_fusion.2), channel_id=1, source_target_pairs={{0,2},{1,3},{2,0},{3,1},{4,6},{5,7},{6,4},{7,5},{8,10},{9,11},{10,... | collective-permute-start | bytes 196616 | tf_op jit(solution)/shard_map/ppermute | solution.py:175
  6.3 0.7 %collective-permute-start.4 = (bf16[256,512]{1,0:T(8,128)(2,1)S(1)}, bf16[256,512]{1,0:T(8,128)(2,1)S(1)}, u32[]{:S(2)}, u32[]{:S(2)}) collective-permute-start(bf16[256,512]{1,0:T(8,128)(2,1)S(1)} %copy-done.3), channel_id=1, source_target_pairs={{3,4},{7,8},{11,12},{15,16},{19,20},{23,24},{27,28},{4,3},{8,7},{1... | collective-permute-start | bytes 786440 | tf_op jit(solution)/shard_map/ppermute | solution.py:244
  7.0 5.2 %collective-permute-done.3.across_ref = bf16[256,512]{1,0:T(8,128)(2,1)S(1)} collective-permute-done((bf16[256,512]{1,0:T(8,128)(2,1)S(1)}, bf16[256,512]{1,0:T(8,128)(2,1)S(1)}, u32[]{:S(2)}, u32[]{:S(2)}) %collective-permute-start.3) | collective-permute-done | bytes 262176 | tf_op jit(solution)/shard_map/ppermute | solution.py:175
  12.2 0.0 collective-permute-start.5
  12.2 0.5 %collective-permute-start.2 = (bf16[256,512]{1,0:T(8,128)(2,1)S(1)}, bf16[256,512]{1,0:T(8,128)(2,1)S(1)}, u32[]{:S(2)}, u32[]{:S(2)}) collective-permute-start(bf16[256,512]{1,0:T(8,128)(2,1)S(1)} %copy-done.3), channel_id=1, source_target_pairs={{0,1},{1,0},{2,3},{3,2},{4,5},{5,4},{6,7},{7,6},{8,9},{9,8},{10,11... | collective-permute-start | bytes 786440 | tf_op jit(solution)/shard_map/ppermute | solution.py:175
  12.7 0.7 %collective-permute-start.7 = (s32[1,4]{1,0:T(1,128)S(1)}, s32[1,4]{1,0:T(1,128)S(1)}, u32[]{:S(2)}, u32[]{:S(2)}) collective-permute-start(s32[1,4]{1,0:T(1,128)S(1)} %copy-done.2), channel_id=1, source_target_pairs={{4,8},{12,16},{20,24},{8,4},{16,12},{24,20},{5,9},{13,17},{21,25},... | collective-permute-start | bytes 56 | tf_op jit(solution)/shard_map/ppermute | solution.py:192
  13.4 2.1 %collective-permute-done.1 = bf16[128,256]{1,0:T(8,128)(2,1)S(1)} collective-permute-done((bf16[128,256]{1,0:T(8,128)(2,1)S(1)}, bf16[128,256]{1,0:T(8,128)(2,1)S(1)}, u32[]{:S(2)}, u32[]{:S(2)}) %collective-permute-start.1) | collective-permute-done | bytes 65568 | tf_op jit(solution)/shard_map/ppermute | solution.py:175
  15.5 2.8 %collective-permute-start.6 = (s32[1,4]{1,0:T(1,128)S(1)}, s32[1,4]{1,0:T(1,128)S(1)}, u32[]{:S(2)}, u32[]{:S(2)}) collective-permute-start(s32[1,4]{1,0:T(1,128)S(1)} %copy-done.2), channel_id=1, source_target_pairs={{0,4},{8,12},{16,20},{24,28},{4,0},{12,8},{20,16},{28,24},{1,5},{9... | collective-permute-start | bytes 56 | tf_op jit(solution)/shard_map/ppermute | solution.py:192
  18.3 0.0 collective-permute-done.5.corner_ref
  18.3 0.0 collective-permute-done.7.odd_cols
  18.3 1.5 %collective-permute-done.6.even_cols = s32[1,4]{1,0:T(1,128)S(1)} collective-permute-done((s32[1,4]{1,0:T(1,128)S(1)}, s32[1,4]{1,0:T(1,128)S(1)}, u32[]{:S(2)}, u32[]{:S(2)}) %collective-permute-start.6) | collective-permute-done | bytes 48 | tf_op jit(solution)/shard_map/ppermute | solution.py:192
  19.7 0.0 collective-permute-done.2.mate_ref
  19.7 0.6 %pick.1 = (bf16[256,512]{1,0:T(8,128)(2,1)S(1)}, bf16[256,512]{1,0:T(8,128)(2,1)S(1)}) custom-call(bf16[256,512]{1,0:T(8,128)(2,1)S(1)} %get-tuple-element.25.x_ref, bf16[256,512]{1,0:T(8,128)(2,1)S(1)} %collective-permute-done.2.mate_ref, bf16[256,512]{1,0:T(8,128)(2,1)S(1)} %collective-permute-done.3.across_ref, ...), custom_call_target="tpu_custom_call" | custom-call | tf_op jit(solution)/shard_map/pick/pallas_call | solution.py:29
  20.4 0.0 copy-start.1
  20.4 2.1 %collective-permute-start.8 = (bf16[128,256]{1,0:T(8,128)(2,1)S(1)}, bf16[128,256]{1,0:T(8,128)(2,1)S(1)}, u32[]{:S(2)}, u32[]{:S(2)}) collective-permute-start(bf16[128,256]{1,0:T(8,128)(2,1)S(1)} %add_convert_fusion.1.own_ref), channel_id=1, source_target_pairs={{0,4},{4,0},{8,12},{12,8},{16,20},{20,16},{24,28},{28,24},{1,5},{5... | collective-permute-start | bytes 196616 | tf_op jit(solution)/shard_map/ppermute | solution.py:186
  23.1 1.1 %near.1.acc_ref = f32[256,512]{1,0:T(8,128)S(1)} custom-call(bf16[256,512]{1,0:T(8,128)(2,1)S(1)} %get-tuple-element.25.x_ref, bf16[256,512]{1,0:T(8,128)(2,1)S(1)} %collective-permute-done.2.mate_ref, bf16[256,512]{1,0:T(8,128)(2,1)S(1)} %collective-permute-done.3.across_ref, bf16[256,512]{1,0:T(8,128)(2,1)S(1)} %collective-permute-done.5.corner_ref, ...), custom_call_target="tpu_custom_call" | custom-call | tf_op jit(solution)/shard_map/near/pallas_call | solution.py:29
  24.3 0.4 collective-permute-done.8.mate_ref
  24.7 2.4 %push.1 = (bf16[128,256]{1,0:T(8,128)(2,1)S(1)}, bf16[128,256]{1,0:T(8,128)(2,1)S(1)}, bf16[128,256]{1,0:T(8,128)(2,1)S(1)}, bf16[128,256]{1,0:T(8,128)(2,1)}) custom-call(bf16[128,256]{1,0:T(8,128)(2,1)S(1)} %add_convert_fusion.1.own_ref, bf16[128,256]{1,0:T(8,128)(2,1)S(1)} %collective-permute-done.8.mate_ref, ...), custom_call_target="tpu_custom_call" | custom-call | tf_op jit(solution)/shard_map/push/pallas_call | solution.py:29
  27.1 3.5 %collective-permute-start.11 = (bf16[128,256]{1,0:T(8,128)(2,1)S(1)}, bf16[128,256]{1,0:T(8,128)(2,1)S(1)}, u32[]{:S(2)}, u32[]{:S(2)}) collective-permute-start(bf16[128,256]{1,0:T(8,128)(2,1)S(1)} %get-tuple-element.38), channel_id=1, source_target_pairs={{0,8},{4,12},{8,0},{12,4},{16,24},{20,28},{24,16},{28,20},{1,9},{5... | collective-permute-start | bytes 196616 | tf_op jit(solution)/shard_map/ppermute | solution.py:287
  30.6 3.8 %collective-permute-start.12 = (bf16[128,256]{1,0:T(8,128)(2,1)S(1)}, bf16[128,256]{1,0:T(8,128)(2,1)S(1)}, u32[]{:S(2)}, u32[]{:S(2)}) collective-permute-start(bf16[128,256]{1,0:T(8,128)(2,1)S(1)} %get-tuple-element.39), channel_id=1, source_target_pairs={{0,16},{4,20},{8,24},{12,28},{16,0},{20,4},{24,8},{28,12},{1,17},{... | collective-permute-start | bytes 196616 | tf_op jit(solution)/shard_map/ppermute | solution.py:287
  34.4 0.0 collective-permute-start.13
  34.4 0.7 %collective-permute-start.9 = (bf16[256,512]{1,0:T(8,128)(2,1)S(1)}, bf16[256,512]{1,0:T(8,128)(2,1)S(1)}, u32[]{:S(2)}, u32[]{:S(2)}) collective-permute-start(bf16[256,512]{1,0:T(8,128)(2,1)S(1)} %get-tuple-element.32), channel_id=1, source_target_pairs={{0,4},{8,12},{16,20},{24,28},{4,0},{12,8},{20,16},{28,24},{1,5},{9... | collective-permute-start | bytes 786440 | tf_op jit(solution)/shard_map/ppermute | solution.py:192
  35.1 0.7 %collective-permute-start.10 = (bf16[256,512]{1,0:T(8,128)(2,1)S(1)}, bf16[256,512]{1,0:T(8,128)(2,1)S(1)}, u32[]{:S(2)}, u32[]{:S(2)}) collective-permute-start(bf16[256,512]{1,0:T(8,128)(2,1)S(1)} %get-tuple-element.33), channel_id=1, source_target_pairs={{4,8},{12,16},{20,24},{8,4},{16,12},{24,20},{5,9},{13,17},{21,25},... | collective-permute-start | bytes 786440 | tf_op jit(solution)/shard_map/ppermute | solution.py:192
  35.8 2.3 %collective-permute-done.12 = bf16[128,256]{1,0:T(8,128)(2,1)S(1)} collective-permute-done((bf16[128,256]{1,0:T(8,128)(2,1)S(1)}, bf16[128,256]{1,0:T(8,128)(2,1)S(1)}, u32[]{:S(2)}, u32[]{:S(2)}) %collective-permute-start.12) | collective-permute-done | bytes 65568 | tf_op jit(solution)/shard_map/ppermute | solution.py:287
  38.1 3.1 %collective-permute-done.13 = bf16[128,256]{1,0:T(8,128)(2,1)S(1)} collective-permute-done((bf16[128,256]{1,0:T(8,128)(2,1)S(1)}, bf16[128,256]{1,0:T(8,128)(2,1)S(1)}, u32[]{:S(2)}, u32[]{:S(2)}) %collective-permute-start.13) | collective-permute-done | bytes 65568 | tf_op jit(solution)/shard_map/ppermute | solution.py:287
  41.3 0.1 collective-permute-start.14
  41.3 1.2 %collective-permute-done.14.mate_field = bf16[128,256]{1,0:T(8,128)(2,1)S(1)} collective-permute-done((bf16[128,256]{1,0:T(8,128)(2,1)S(1)}, bf16[128,256]{1,0:T(8,128)(2,1)S(1)}, u32[]{:S(2)}, u32[]{:S(2)}) %collective-permute-start.14) | collective-permute-done | bytes 65568 | tf_op jit(solution)/shard_map/ppermute | solution.py:175
  42.6 1.9 %collective-permute-done.9.even_ref = bf16[256,512]{1,0:T(8,128)(2,1)S(1)} collective-permute-done((bf16[256,512]{1,0:T(8,128)(2,1)S(1)}, bf16[256,512]{1,0:T(8,128)(2,1)S(1)}, u32[]{:S(2)}, u32[]{:S(2)}) %collective-permute-start.9) | collective-permute-done | bytes 262176 | tf_op jit(solution)/shard_map/ppermute | solution.py:192
  44.5 1.8 %finish.1 = bf16[256,512]{1,0:T(8,128)(2,1)} custom-call(f32[256,512]{1,0:T(8,128)S(1)} %near.1.acc_ref, bf16[256,512]{1,0:T(8,128)(2,1)S(1)} %collective-permute-done.9.even_ref, bf16[256,512]{1,0:T(8,128)(2,1)S(1)} %collective-permute-done.10.odd_ref, bf16[1,4,512,512]{3,2,1,0:T(8,128)(2,1)S(1)} %copy-done, bf16[512,256]{1,0:T(8,128)(2,1)S(1)} %get-tuple-element.34.w_ref, ...), custom_call_target="tpu_custom_call" | custom-call | tf_op jit(solution)/shard_map/finish/pallas_call | solution.py:29
  (14 shorter events, 0.1 us)
Async XLA Ops:
  0.0 2.5 %copy-start.3 = (bf16[256,512]{1,0:T(8,128)(2,1)S(1)}, bf16[256,512]{1,0:T(8,128)(2,1)}, u32[]{:S(2)}) copy-start(bf16[256,512]{1,0:T(8,128)(2,1)} %x_hbm.1) | copy-start | bytes 786436
  0.0 12.7 %copy-start.2 = (s32[1,4]{1,0:T(1,128)S(1)}, s32[1,4]{1,0:T(1,128)}, u32[]{:S(2)}) copy-start(s32[1,4]{1,0:T(1,128)} %cols_ref.3) | copy-start | bytes 52
  0.0 23.1 %copy-start = (bf16[1,4,512,512]{3,2,1,0:T(8,128)(2,1)S(1)}, bf16[1,4,512,512]{3,2,1,0:T(8,128)(2,1)}, u32[]{:S(2)}) copy-start(bf16[1,4,512,512]{3,2,1,0:T(8,128)(2,1)} %tiles_ref.3) | copy-start | bytes 6291460
  2.0 3.1 %collective-permute-start = (bf16[128,256]{1,0:T(8,128)(2,1)S(1)}, bf16[128,256]{1,0:T(8,128)(2,1)S(1)}, u32[]{:S(2)}, u32[]{:S(2)}) collective-permute-start(bf16[128,256]{1,0:T(8,128)(2,1)S(1)} %get-tuple-element.24), channel_id=1, source_target_pairs={{0,1},{1,0},{2,3},{3,2},{4,5},{5,4},{6,7},{7,6},{8,9},{9,8},{10,11... | collective-permute-start | bytes 196616 | tf_op jit(solution)/shard_map/ppermute | solution.py:175
  2.5 9.7 %collective-permute-start.3 = (bf16[256,512]{1,0:T(8,128)(2,1)S(1)}, bf16[256,512]{1,0:T(8,128)(2,1)S(1)}, u32[]{:S(2)}, u32[]{:S(2)}) collective-permute-start(bf16[256,512]{1,0:T(8,128)(2,1)S(1)} %copy-done.3), channel_id=1, source_target_pairs={{0,2},{1,3},{2,0},{3,1},{4,6},{5,7},{6,4},{7,5},{8,10},{9,11},{10,... | collective-permute-start | bytes 786440 | tf_op jit(solution)/shard_map/ppermute | solution.py:175
  5.1 10.4 %collective-permute-start.1 = (bf16[128,256]{1,0:T(8,128)(2,1)S(1)}, bf16[128,256]{1,0:T(8,128)(2,1)S(1)}, u32[]{:S(2)}, u32[]{:S(2)}) collective-permute-start(bf16[128,256]{1,0:T(8,128)(2,1)S(1)} %add_convert_fusion.2), channel_id=1, source_target_pairs={{0,2},{1,3},{2,0},{3,1},{4,6},{5,7},{6,4},{7,5},{8,10},{9,11},{10,... | collective-permute-start | bytes 196616 | tf_op jit(solution)/shard_map/ppermute | solution.py:175
  6.3 11.9 %collective-permute-start.4 = (bf16[256,512]{1,0:T(8,128)(2,1)S(1)}, bf16[256,512]{1,0:T(8,128)(2,1)S(1)}, u32[]{:S(2)}, u32[]{:S(2)}) collective-permute-start(bf16[256,512]{1,0:T(8,128)(2,1)S(1)} %copy-done.3), channel_id=1, source_target_pairs={{3,4},{7,8},{11,12},{15,16},{19,20},{23,24},{27,28},{4,3},{8,7},{1... | collective-permute-start | bytes 786440 | tf_op jit(solution)/shard_map/ppermute | solution.py:244
  12.2 6.0 %collective-permute-start.5 = (bf16[256,512]{1,0:T(8,128)(2,1)S(1)}, bf16[256,512]{1,0:T(8,128)(2,1)S(1)}, u32[]{:S(2)}, u32[]{:S(2)}) collective-permute-start(bf16[256,512]{1,0:T(8,128)(2,1)S(1)} %collective-permute-done.3.across_ref), channel_id=1, source_target_pairs={{0,1},{1,0},{2,3},{3,2},{4,5},{5,4},{6,7},{7,6},{8,9},{9,8},{10,11... | collective-permute-start | bytes 786440 | tf_op jit(solution)/shard_map/ppermute | solution.py:175
  12.2 7.5 %collective-permute-start.2 = (bf16[256,512]{1,0:T(8,128)(2,1)S(1)}, bf16[256,512]{1,0:T(8,128)(2,1)S(1)}, u32[]{:S(2)}, u32[]{:S(2)}) collective-permute-start(bf16[256,512]{1,0:T(8,128)(2,1)S(1)} %copy-done.3), channel_id=1, source_target_pairs={{0,1},{1,0},{2,3},{3,2},{4,5},{5,4},{6,7},{7,6},{8,9},{9,8},{10,11... | collective-permute-start | bytes 786440 | tf_op jit(solution)/shard_map/ppermute | solution.py:175
  12.7 5.5 %collective-permute-start.7 = (s32[1,4]{1,0:T(1,128)S(1)}, s32[1,4]{1,0:T(1,128)S(1)}, u32[]{:S(2)}, u32[]{:S(2)}) collective-permute-start(s32[1,4]{1,0:T(1,128)S(1)} %copy-done.2), channel_id=1, source_target_pairs={{4,8},{12,16},{20,24},{8,4},{16,12},{24,20},{5,9},{13,17},{21,25},... | collective-permute-start | bytes 56 | tf_op jit(solution)/shard_map/ppermute | solution.py:192
  15.5 4.3 %collective-permute-start.6 = (s32[1,4]{1,0:T(1,128)S(1)}, s32[1,4]{1,0:T(1,128)S(1)}, u32[]{:S(2)}, u32[]{:S(2)}) collective-permute-start(s32[1,4]{1,0:T(1,128)S(1)} %copy-done.2), channel_id=1, source_target_pairs={{0,4},{8,12},{16,20},{24,28},{4,0},{12,8},{20,16},{28,24},{1,5},{9... | collective-permute-start | bytes 56 | tf_op jit(solution)/shard_map/ppermute | solution.py:192
  20.4 4.3 %copy-start.1 = (s32[6,8,2]{1,2,0:T(2,128)S(1)}, s32[6,8,2]{1,2,0:T(2,128)}, u32[]{:S(2)}) copy-start(s32[6,8,2]{1,2,0:T(2,128)} %param.15) | copy-start | bytes 1156
  20.4 4.3 %collective-permute-start.8 = (bf16[128,256]{1,0:T(8,128)(2,1)S(1)}, bf16[128,256]{1,0:T(8,128)(2,1)S(1)}, u32[]{:S(2)}, u32[]{:S(2)}) collective-permute-start(bf16[128,256]{1,0:T(8,128)(2,1)S(1)} %add_convert_fusion.1.own_ref), channel_id=1, source_target_pairs={{0,4},{4,0},{8,12},{12,8},{16,20},{20,16},{24,28},{28,24},{1,5},{5... | collective-permute-start | bytes 196616 | tf_op jit(solution)/shard_map/ppermute | solution.py:186
  27.1 8.7 %collective-permute-start.11 = (bf16[128,256]{1,0:T(8,128)(2,1)S(1)}, bf16[128,256]{1,0:T(8,128)(2,1)S(1)}, u32[]{:S(2)}, u32[]{:S(2)}) collective-permute-start(bf16[128,256]{1,0:T(8,128)(2,1)S(1)} %get-tuple-element.38), channel_id=1, source_target_pairs={{0,8},{4,12},{8,0},{12,4},{16,24},{20,28},{24,16},{28,20},{1,9},{5... | collective-permute-start | bytes 196616 | tf_op jit(solution)/shard_map/ppermute | solution.py:287
  30.6 7.4 %collective-permute-start.12 = (bf16[128,256]{1,0:T(8,128)(2,1)S(1)}, bf16[128,256]{1,0:T(8,128)(2,1)S(1)}, u32[]{:S(2)}, u32[]{:S(2)}) collective-permute-start(bf16[128,256]{1,0:T(8,128)(2,1)S(1)} %get-tuple-element.39), channel_id=1, source_target_pairs={{0,16},{4,20},{8,24},{12,28},{16,0},{20,4},{24,8},{28,12},{1,17},{... | collective-permute-start | bytes 196616 | tf_op jit(solution)/shard_map/ppermute | solution.py:287
  34.4 6.8 %collective-permute-start.13 = (bf16[128,256]{1,0:T(8,128)(2,1)S(1)}, bf16[128,256]{1,0:T(8,128)(2,1)S(1)}, u32[]{:S(2)}, u32[]{:S(2)}) collective-permute-start(bf16[128,256]{1,0:T(8,128)(2,1)S(1)} %get-tuple-element.40), channel_id=1, source_target_pairs={{0,24},{4,28},{8,16},{12,20},{16,8},{20,12},{24,0},{28,4},{1,25},{... | collective-permute-start | bytes 196616 | tf_op jit(solution)/shard_map/ppermute | solution.py:287
  34.4 10.1 %collective-permute-start.9 = (bf16[256,512]{1,0:T(8,128)(2,1)S(1)}, bf16[256,512]{1,0:T(8,128)(2,1)S(1)}, u32[]{:S(2)}, u32[]{:S(2)}) collective-permute-start(bf16[256,512]{1,0:T(8,128)(2,1)S(1)} %get-tuple-element.32), channel_id=1, source_target_pairs={{0,4},{8,12},{16,20},{24,28},{4,0},{12,8},{20,16},{28,24},{1,5},{9... | collective-permute-start | bytes 786440 | tf_op jit(solution)/shard_map/ppermute | solution.py:192
  35.1 9.4 %collective-permute-start.10 = (bf16[256,512]{1,0:T(8,128)(2,1)S(1)}, bf16[256,512]{1,0:T(8,128)(2,1)S(1)}, u32[]{:S(2)}, u32[]{:S(2)}) collective-permute-start(bf16[256,512]{1,0:T(8,128)(2,1)S(1)} %get-tuple-element.33), channel_id=1, source_target_pairs={{4,8},{12,16},{20,24},{8,4},{16,12},{24,20},{5,9},{13,17},{21,25},... | collective-permute-start | bytes 786440 | tf_op jit(solution)/shard_map/ppermute | solution.py:192
  41.3 1.3 %collective-permute-start.14 = (bf16[128,256]{1,0:T(8,128)(2,1)S(1)}, bf16[128,256]{1,0:T(8,128)(2,1)S(1)}, u32[]{:S(2)}, u32[]{:S(2)}) collective-permute-start(bf16[128,256]{1,0:T(8,128)(2,1)S(1)} %add_convert_fusion.own_field), channel_id=1, source_target_pairs={{0,1},{1,0},{2,3},{3,2},{4,5},{5,4},{6,7},{7,6},{8,9},{9,8},{10,11... | collective-permute-start | bytes 196616 | tf_op jit(solution)/shard_map/ppermute | solution.py:175

commit v3 on v2

--- a/solution.py
+++ b/solution.py
@@ -238,13 +238,17 @@
     half = ((rows, rank), BF16)
     cube = 2 * rank * rank
 
+    even_cols = neighbours(near_cols, 0)
+    odd_cols = neighbours(near_cols, 1)
     across = turned(points_x, 2)
     mate = turned(points_x, 1)
+    sent, across, even_cols, odd_cols = lax.optimization_barrier(
+        (points_x, across, even_cols, odd_cols)
+    )
     joints = [(GROUP * g - 1, GROUP * g) for g in range(1, leaf_count)]
-    edge = lax.ppermute(points_x, ("leaf", "level"), joints + [(b, a) for a, b in joints])
-    even_cols = neighbours(near_cols, 0)
-    odd_cols = neighbours(near_cols, 1)
+    edge = lax.ppermute(sent, ("leaf", "level"), joints + [(b, a) for a, b in joints])
     corner = turned(across, 1)
+    edge, corner = lax.optimization_barrier((edge, corner))
 
     keep, send, w, own_x, transfer_in, coupling_in = call(
         partial(up_kernel, bits), "up", cube * (vectors + bits * points) * 2,
@@ -257,12 +261,10 @@
     )
     coef = (keep.astype(F32) + turned(send, 1).astype(F32)).astype(BF16)
     coef = (coef.astype(F32) + turned(coef, 2).astype(F32)).astype(BF16)
-    edge, corner = lax.optimization_barrier((edge, corner))
+    beside = swapped(coef, 0)
     to_even, to_odd = call(
         pick_kernel, "pick", 0, [own_x, mate, across, corner], [even_cols, odd_cols], [block] * 2
     )
-    coef, to_even, to_odd = lax.optimization_barrier((coef, to_even, to_odd))
-    beside = swapped(coef, 0)
     from_even = neighbours(to_even, 0)
     from_odd = neighbours(to_odd, 1)
 
@@ -271,7 +273,6 @@
         [own_x, mate, across, corner, edge, near_tiles], [near_cols, near_count],
         [((vectors, points), F32)],
     )
-    beside, acc = lax.optimization_barrier((beside, acc))
     active = min(coupling.shape[0], leaf_count.bit_length())
     pairs = leaf_count // 2
     turns = [1, 2, 3] if pairs == 4 else [1, 2, 3, -1, -2, -3]

time: 46.4 us -> 41.5 us (0.89)
  the two profiles are of different devices: /device:TPU:0 before, /device:TPU:4 now
where the time goes in v3:
time: 41.5 us; the launch traced here: 41.2 us
  starting transfers between devices  19.6 us (47%)
  waiting for transfers between devices  13 us (31%)
  Pallas kernels  7.66 us (18%)
  between operations  0.82 us (2%)
    ppermute x4, starting transfers between devices, neighbours(): return lax.ppermute(value, 'leaf', route + [(b, a) for a, b in route])  9.14 us
    pallas_call x5, Pallas kernels, call(): pl.pallas_call(kernel, out_shape=shapes, in_specs=[pl.BlockSpec(memory_sp...  7.66 us
    ppermute x1, waiting for transfers between devices, swapped(): lax.ppermute(value, 'leaf', [(i, i ^ 1 << distance) for i in range(count)])  6.18 us
    ppermute x4, waiting for transfers between devices, neighbours(): return lax.ppermute(value, 'leaf', route + [(b, a) for a, b in route])  6.15 us
    ppermute x3, starting transfers between devices, per_device(): lax.ppermute(push, 'leaf', [(i, i ^ 2 * turn) for i in range(leaf_count)])  4.39 us
    ppermute x6, starting transfers between devices, turned(): return lax.ppermute(value, 'level', [(i, i ^ turn) for i in range(GROUP)])  3 us
    ppermute x1, starting transfers between devices, per_device(): lax.ppermute(sent, ('leaf', 'level'), joints + [(b, a) for a, b in joints])  2.97 us
  transfers between devices with their start and end apart: 15, of which 5 were waited for; matrix products, arithmetic and copies ran while one was open for 0% of the time, Pallas kernels for 10%

profile of v3, /device:TPU:4, one launch (start us, length us, event | category | flops | bytes accessed | tf_op | source)
XLA Modules:
  0.0 41.2 jit_solution(13407820147112128932)
XLA Ops:
  0.0 2.0 %up.1 = (bf16[128,256]{1,0:T(8,128)(2,1)S(1)}, bf16[128,256]{1,0:T(8,128)(2,1)S(1)}, bf16[512,256]{1,0:T(8,128)(2,1)S(1)}, bf16[256,512]{1,0:T(8,128)(2,1)S(1)},...) custom-call(bf16[256,512]{1,0:T(8,128)(2,1)} %x_hbm.1, bf16[1,512,256]{2,1,0:T(8,128)(2,1)} %basis_hbm.1, ...), custom_call_target="tpu_custom_call" | custom-call | tf_op jit(solution)/shard_map/up/pallas_call | solution.py:29
  2.0 0.1 collective-permute-start.8
  2.1 1.6 %collective-permute-start.1 = (bf16[256,512]{1,0:T(8,128)(2,1)S(1)}, bf16[256,512]{1,0:T(8,128)(2,1)S(1)}, u32[]{:S(2)}, u32[]{:S(2)}) collective-permute-start(bf16[256,512]{1,0:T(8,128)(2,1)S(1)} %copy-done.3), channel_id=1, source_target_pairs={{0,2},{1,3},{2,0},{3,1},{4,6},{5,7},{6,4},{7,5},{8,10},{9,11},{10,... | collective-permute-start | bytes 786440 | tf_op jit(solution)/shard_map/ppermute | solution.py:175
  3.6 0.0 collective-permute-done.8
  3.7 1.2 %collective-permute-start.9 = (bf16[128,256]{1,0:T(8,128)(2,1)S(1)}, bf16[128,256]{1,0:T(8,128)(2,1)S(1)}, u32[]{:S(2)}, u32[]{:S(2)}) collective-permute-start(bf16[128,256]{1,0:T(8,128)(2,1)S(1)} %add_convert_fusion.2), channel_id=1, source_target_pairs={{0,2},{1,3},{2,0},{3,1},{4,6},{5,7},{6,4},{7,5},{8,10},{9,11},{10,... | collective-permute-start | bytes 196616 | tf_op jit(solution)/shard_map/ppermute | solution.py:175
  4.9 0.5 %collective-permute-start.2 = (s32[1,4]{1,0:T(1,128)S(1)}, s32[1,4]{1,0:T(1,128)S(1)}, u32[]{:S(2)}, u32[]{:S(2)}) collective-permute-start(s32[1,4]{1,0:T(1,128)S(1)} %copy-done.2), channel_id=1, source_target_pairs={{0,4},{8,12},{16,20},{24,28},{4,0},{12,8},{20,16},{28,24},{1,5},{9... | collective-permute-start | bytes 56 | tf_op jit(solution)/shard_map/ppermute | solution.py:192
  5.4 4.4 %collective-permute-start.3 = (s32[1,4]{1,0:T(1,128)S(1)}, s32[1,4]{1,0:T(1,128)S(1)}, u32[]{:S(2)}, u32[]{:S(2)}) collective-permute-start(s32[1,4]{1,0:T(1,128)S(1)} %copy-done.2), channel_id=1, source_target_pairs={{4,8},{12,16},{20,24},{8,4},{16,12},{24,20},{5,9},{13,17},{21,25},... | collective-permute-start | bytes 56 | tf_op jit(solution)/shard_map/ppermute | solution.py:192
  9.8 0.1 collective-permute-start
  9.9 0.0 collective-permute-done.2.even_cols
  9.9 1.8 %collective-permute-done.3.odd_cols = s32[1,4]{1,0:T(1,128)S(1)} collective-permute-done((s32[1,4]{1,0:T(1,128)S(1)}, s32[1,4]{1,0:T(1,128)S(1)}, u32[]{:S(2)}, u32[]{:S(2)}) %collective-permute-start.3) | collective-permute-done | bytes 48 | tf_op jit(solution)/shard_map/ppermute | solution.py:192
  11.7 0.0 collective-permute-done.1.across_ref
  11.7 0.0 collective-permute-start.5
  11.7 3.0 %collective-permute-start.4 = (bf16[256,512]{1,0:T(8,128)(2,1)S(1)}, bf16[256,512]{1,0:T(8,128)(2,1)S(1)}, u32[]{:S(2)}, u32[]{:S(2)}) collective-permute-start(bf16[256,512]{1,0:T(8,128)(2,1)S(1)} %copy-done.3), channel_id=1, source_target_pairs={{3,4},{7,8},{11,12},{15,16},{19,20},{23,24},{27,28},{4,3},{8,7},{1... | collective-permute-start | bytes 786440 | tf_op jit(solution)/shard_map/ppermute | solution.py:249
  14.7 0.0 collective-permute-done.9
  14.7 0.1 collective-permute-start.10
  14.8 6.2 %collective-permute-done.10.mate_ref = bf16[128,256]{1,0:T(8,128)(2,1)S(1)} collective-permute-done((bf16[128,256]{1,0:T(8,128)(2,1)S(1)}, bf16[128,256]{1,0:T(8,128)(2,1)S(1)}, u32[]{:S(2)}, u32[]{:S(2)}) %collective-permute-start.10) | collective-permute-done | bytes 65568 | tf_op jit(solution)/shard_map/ppermute | solution.py:186
  21.0 2.4 %push.1 = (bf16[128,256]{1,0:T(8,128)(2,1)S(1)}, bf16[128,256]{1,0:T(8,128)(2,1)S(1)}, bf16[128,256]{1,0:T(8,128)(2,1)S(1)}, bf16[128,256]{1,0:T(8,128)(2,1)}) custom-call(bf16[128,256]{1,0:T(8,128)(2,1)S(1)} %add_convert_fusion.1.own_ref, bf16[128,256]{1,0:T(8,128)(2,1)S(1)} %collective-permute-done.10.mate_ref, ...), custom_call_target="tpu_custom_call" | custom-call | tf_op jit(solution)/shard_map/push/pallas_call | solution.py:29
  23.4 1.4 %collective-permute-start.11 = (bf16[128,256]{1,0:T(8,128)(2,1)S(1)}, bf16[128,256]{1,0:T(8,128)(2,1)S(1)}, u32[]{:S(2)}, u32[]{:S(2)}) collective-permute-start(bf16[128,256]{1,0:T(8,128)(2,1)S(1)} %get-tuple-element.36), channel_id=1, source_target_pairs={{0,8},{4,12},{8,0},{12,4},{16,24},{20,28},{24,16},{28,20},{1,9},{5... | collective-permute-start | bytes 196616 | tf_op jit(solution)/shard_map/ppermute | solution.py:288
  24.8 2.5 %collective-permute-start.12 = (bf16[128,256]{1,0:T(8,128)(2,1)S(1)}, bf16[128,256]{1,0:T(8,128)(2,1)S(1)}, u32[]{:S(2)}, u32[]{:S(2)}) collective-permute-start(bf16[128,256]{1,0:T(8,128)(2,1)S(1)} %get-tuple-element.37), channel_id=1, source_target_pairs={{0,16},{4,20},{8,24},{12,28},{16,0},{20,4},{24,8},{28,12},{1,17},{... | collective-permute-start | bytes 196616 | tf_op jit(solution)/shard_map/ppermute | solution.py:288
  27.3 0.0 collective-permute-done.5.corner_ref
  27.3 0.5 %collective-permute-start.13 = (bf16[128,256]{1,0:T(8,128)(2,1)S(1)}, bf16[128,256]{1,0:T(8,128)(2,1)S(1)}, u32[]{:S(2)}, u32[]{:S(2)}) collective-permute-start(bf16[128,256]{1,0:T(8,128)(2,1)S(1)} %get-tuple-element.38), channel_id=1, source_target_pairs={{0,24},{4,28},{8,16},{12,20},{16,8},{20,12},{24,0},{28,4},{1,25},{... | collective-permute-start | bytes 196616 | tf_op jit(solution)/shard_map/ppermute | solution.py:288
  27.8 0.6 %pick.1 = (bf16[256,512]{1,0:T(8,128)(2,1)S(1)}, bf16[256,512]{1,0:T(8,128)(2,1)S(1)}) custom-call(bf16[256,512]{1,0:T(8,128)(2,1)S(1)} %get-tuple-element.22.x_ref, bf16[256,512]{1,0:T(8,128)(2,1)S(1)} %collective-permute-done.mate_ref, bf16[256,512]{1,0:T(8,128)(2,1)S(1)} %collective-permute-done.1.across_ref, ...), custom_call_target="tpu_custom_call" | custom-call | tf_op jit(solution)/shard_map/pick/pallas_call | solution.py:29
  28.4 2.0 %collective-permute-start.6 = (bf16[256,512]{1,0:T(8,128)(2,1)S(1)}, bf16[256,512]{1,0:T(8,128)(2,1)S(1)}, u32[]{:S(2)}, u32[]{:S(2)}) collective-permute-start(bf16[256,512]{1,0:T(8,128)(2,1)S(1)} %get-tuple-element.29), channel_id=1, source_target_pairs={{0,4},{8,12},{16,20},{24,28},{4,0},{12,8},{20,16},{28,24},{1,5},{9... | collective-permute-start | bytes 786440 | tf_op jit(solution)/shard_map/ppermute | solution.py:192
  30.5 2.2 %collective-permute-start.7 = (bf16[256,512]{1,0:T(8,128)(2,1)S(1)}, bf16[256,512]{1,0:T(8,128)(2,1)S(1)}, u32[]{:S(2)}, u32[]{:S(2)}) collective-permute-start(bf16[256,512]{1,0:T(8,128)(2,1)S(1)} %get-tuple-element.30), channel_id=1, source_target_pairs={{4,8},{12,16},{20,24},{8,4},{16,12},{24,20},{5,9},{13,17},{21,25},... | collective-permute-start | bytes 786440 | tf_op jit(solution)/shard_map/ppermute | solution.py:192
  32.7 0.0 collective-permute-done.12
  32.7 0.7 %collective-permute-done.13 = bf16[128,256]{1,0:T(8,128)(2,1)S(1)} collective-permute-done((bf16[128,256]{1,0:T(8,128)(2,1)S(1)}, bf16[128,256]{1,0:T(8,128)(2,1)S(1)}, u32[]{:S(2)}, u32[]{:S(2)}) %collective-permute-start.13) | collective-permute-done | bytes 65568 | tf_op jit(solution)/shard_map/ppermute | solution.py:288
  33.4 0.1 collective-permute-start.14
  34.1 1.1 %near.1.acc_ref = f32[256,512]{1,0:T(8,128)S(1)} custom-call(bf16[256,512]{1,0:T(8,128)(2,1)S(1)} %get-tuple-element.22.x_ref, bf16[256,512]{1,0:T(8,128)(2,1)S(1)} %collective-permute-done.mate_ref, bf16[256,512]{1,0:T(8,128)(2,1)S(1)} %collective-permute-done.1.across_ref, bf16[256,512]{1,0:T(8,128)(2,1)S(1)} %collective-permute-done.5.corner_ref, ...), custom_call_target="tpu_custom_call" | custom-call | tf_op jit(solution)/shard_map/near/pallas_call | solution.py:29
  35.3 0.0 collective-permute-done.14.mate_field
  35.3 0.2 collective-permute-done.6.even_ref
  35.5 4.2 %collective-permute-done.7.odd_ref = bf16[256,512]{1,0:T(8,128)(2,1)S(1)} collective-permute-done((bf16[256,512]{1,0:T(8,128)(2,1)S(1)}, bf16[256,512]{1,0:T(8,128)(2,1)S(1)}, u32[]{:S(2)}, u32[]{:S(2)}) %collective-permute-start.7) | collective-permute-done | bytes 262176 | tf_op jit(solution)/shard_map/ppermute | solution.py:192
  39.6 1.5 %finish.1 = bf16[256,512]{1,0:T(8,128)(2,1)} custom-call(f32[256,512]{1,0:T(8,128)S(1)} %near.1.acc_ref, bf16[256,512]{1,0:T(8,128)(2,1)S(1)} %collective-permute-done.6.even_ref, bf16[256,512]{1,0:T(8,128)(2,1)S(1)} %collective-permute-done.7.odd_ref, bf16[1,4,512,512]{3,2,1,0:T(8,128)(2,1)S(1)} %copy-done, bf16[512,256]{1,0:T(8,128)(2,1)S(1)} %get-tuple-element.31.w_ref, ...), custom_call_target="tpu_custom_call" | custom-call | tf_op jit(solution)/shard_map/finish/pallas_call | solution.py:29
  (14 shorter events, 0.1 us)
Async XLA Ops:
  0.0 2.1 %copy-start.3 = (bf16[256,512]{1,0:T(8,128)(2,1)S(1)}, bf16[256,512]{1,0:T(8,128)(2,1)}, u32[]{:S(2)}) copy-start(bf16[256,512]{1,0:T(8,128)(2,1)} %x_hbm.1) | copy-start | bytes 786436
  0.0 4.9 %copy-start.2 = (s32[1,4]{1,0:T(1,128)S(1)}, s32[1,4]{1,0:T(1,128)}, u32[]{:S(2)}) copy-start(s32[1,4]{1,0:T(1,128)} %cols_ref.3) | copy-start | bytes 52
  0.0 21.0 %copy-start.1 = (s32[6,8,2]{1,2,0:T(2,128)S(1)}, s32[6,8,2]{1,2,0:T(2,128)}, u32[]{:S(2)}) copy-start(s32[6,8,2]{1,2,0:T(2,128)} %param.15) | copy-start | bytes 1156
  0.0 34.1 %copy-start = (bf16[1,4,512,512]{3,2,1,0:T(8,128)(2,1)S(1)}, bf16[1,4,512,512]{3,2,1,0:T(8,128)(2,1)}, u32[]{:S(2)}) copy-start(bf16[1,4,512,512]{3,2,1,0:T(8,128)(2,1)} %tiles_ref.3) | copy-start | bytes 6291460
  2.0 1.6 %collective-permute-start.8 = (bf16[128,256]{1,0:T(8,128)(2,1)S(1)}, bf16[128,256]{1,0:T(8,128)(2,1)S(1)}, u32[]{:S(2)}, u32[]{:S(2)}) collective-permute-start(bf16[128,256]{1,0:T(8,128)(2,1)S(1)} %get-tuple-element.33), channel_id=1, source_target_pairs={{0,1},{1,0},{2,3},{3,2},{4,5},{5,4},{6,7},{7,6},{8,9},{9,8},{10,11... | collective-permute-start | bytes 196616 | tf_op jit(solution)/shard_map/ppermute | solution.py:175
  2.1 9.6 %collective-permute-start.1 = (bf16[256,512]{1,0:T(8,128)(2,1)S(1)}, bf16[256,512]{1,0:T(8,128)(2,1)S(1)}, u32[]{:S(2)}, u32[]{:S(2)}) collective-permute-start(bf16[256,512]{1,0:T(8,128)(2,1)S(1)} %copy-done.3), channel_id=1, source_target_pairs={{0,2},{1,3},{2,0},{3,1},{4,6},{5,7},{6,4},{7,5},{8,10},{9,11},{10,... | collective-permute-start | bytes 786440 | tf_op jit(solution)/shard_map/ppermute | solution.py:175
  3.7 11.1 %collective-permute-start.9 = (bf16[128,256]{1,0:T(8,128)(2,1)S(1)}, bf16[128,256]{1,0:T(8,128)(2,1)S(1)}, u32[]{:S(2)}, u32[]{:S(2)}) collective-permute-start(bf16[128,256]{1,0:T(8,128)(2,1)S(1)} %add_convert_fusion.2), channel_id=1, source_target_pairs={{0,2},{1,3},{2,0},{3,1},{4,6},{5,7},{6,4},{7,5},{8,10},{9,11},{10,... | collective-permute-start | bytes 196616 | tf_op jit(solution)/shard_map/ppermute | solution.py:175
  4.9 5.0 %collective-permute-start.2 = (s32[1,4]{1,0:T(1,128)S(1)}, s32[1,4]{1,0:T(1,128)S(1)}, u32[]{:S(2)}, u32[]{:S(2)}) collective-permute-start(s32[1,4]{1,0:T(1,128)S(1)} %copy-done.2), channel_id=1, source_target_pairs={{0,4},{8,12},{16,20},{24,28},{4,0},{12,8},{20,16},{28,24},{1,5},{9... | collective-permute-start | bytes 56 | tf_op jit(solution)/shard_map/ppermute | solution.py:192
  5.4 6.3 %collective-permute-start.3 = (s32[1,4]{1,0:T(1,128)S(1)}, s32[1,4]{1,0:T(1,128)S(1)}, u32[]{:S(2)}, u32[]{:S(2)}) collective-permute-start(s32[1,4]{1,0:T(1,128)S(1)} %copy-done.2), channel_id=1, source_target_pairs={{4,8},{12,16},{20,24},{8,4},{16,12},{24,20},{5,9},{13,17},{21,25},... | collective-permute-start | bytes 56 | tf_op jit(solution)/shard_map/ppermute | solution.py:192
  9.8 18.0 %collective-permute-start = (bf16[256,512]{1,0:T(8,128)(2,1)S(1)}, bf16[256,512]{1,0:T(8,128)(2,1)S(1)}, u32[]{:S(2)}, u32[]{:S(2)}) collective-permute-start(bf16[256,512]{1,0:T(8,128)(2,1)S(1)} %copy-done.3), channel_id=1, source_target_pairs={{0,1},{1,0},{2,3},{3,2},{4,5},{5,4},{6,7},{7,6},{8,9},{9,8},{10,11... | collective-permute-start | bytes 786440 | tf_op jit(solution)/shard_map/ppermute | solution.py:175
  11.7 15.6 %collective-permute-start.5 = (bf16[256,512]{1,0:T(8,128)(2,1)S(1)}, bf16[256,512]{1,0:T(8,128)(2,1)S(1)}, u32[]{:S(2)}, u32[]{:S(2)}) collective-permute-start(bf16[256,512]{1,0:T(8,128)(2,1)S(1)} %collective-permute-done.1.across_ref), channel_id=1, source_target_pairs={{0,1},{1,0},{2,3},{3,2},{4,5},{5,4},{6,7},{7,6},{8,9},{9,8},{10,11... | collective-permute-start | bytes 786440 | tf_op jit(solution)/shard_map/ppermute | solution.py:175
  11.7 16.1 %collective-permute-start.4 = (bf16[256,512]{1,0:T(8,128)(2,1)S(1)}, bf16[256,512]{1,0:T(8,128)(2,1)S(1)}, u32[]{:S(2)}, u32[]{:S(2)}) collective-permute-start(bf16[256,512]{1,0:T(8,128)(2,1)S(1)} %copy-done.3), channel_id=1, source_target_pairs={{3,4},{7,8},{11,12},{15,16},{19,20},{23,24},{27,28},{4,3},{8,7},{1... | collective-permute-start | bytes 786440 | tf_op jit(solution)/shard_map/ppermute | solution.py:249
  14.7 6.3 %collective-permute-start.10 = (bf16[128,256]{1,0:T(8,128)(2,1)S(1)}, bf16[128,256]{1,0:T(8,128)(2,1)S(1)}, u32[]{:S(2)}, u32[]{:S(2)}) collective-permute-start(bf16[128,256]{1,0:T(8,128)(2,1)S(1)} %add_convert_fusion.1.own_ref), channel_id=1, source_target_pairs={{0,4},{4,0},{8,12},{12,8},{16,20},{20,16},{24,28},{28,24},{1,5},{5... | collective-permute-start | bytes 196616 | tf_op jit(solution)/shard_map/ppermute | solution.py:186
  23.4 9.2 %collective-permute-start.11 = (bf16[128,256]{1,0:T(8,128)(2,1)S(1)}, bf16[128,256]{1,0:T(8,128)(2,1)S(1)}, u32[]{:S(2)}, u32[]{:S(2)}) collective-permute-start(bf16[128,256]{1,0:T(8,128)(2,1)S(1)} %get-tuple-element.36), channel_id=1, source_target_pairs={{0,8},{4,12},{8,0},{12,4},{16,24},{20,28},{24,16},{28,20},{1,9},{5... | collective-permute-start | bytes 196616 | tf_op jit(solution)/shard_map/ppermute | solution.py:288
  24.8 7.9 %collective-permute-start.12 = (bf16[128,256]{1,0:T(8,128)(2,1)S(1)}, bf16[128,256]{1,0:T(8,128)(2,1)S(1)}, u32[]{:S(2)}, u32[]{:S(2)}) collective-permute-start(bf16[128,256]{1,0:T(8,128)(2,1)S(1)} %get-tuple-element.37), channel_id=1, source_target_pairs={{0,16},{4,20},{8,24},{12,28},{16,0},{20,4},{24,8},{28,12},{1,17},{... | collective-permute-start | bytes 196616 | tf_op jit(solution)/shard_map/ppermute | solution.py:288
  27.3 6.1 %collective-permute-start.13 = (bf16[128,256]{1,0:T(8,128)(2,1)S(1)}, bf16[128,256]{1,0:T(8,128)(2,1)S(1)}, u32[]{:S(2)}, u32[]{:S(2)}) collective-permute-start(bf16[128,256]{1,0:T(8,128)(2,1)S(1)} %get-tuple-element.38), channel_id=1, source_target_pairs={{0,24},{4,28},{8,16},{12,20},{16,8},{20,12},{24,0},{28,4},{1,25},{... | collective-permute-start | bytes 196616 | tf_op jit(solution)/shard_map/ppermute | solution.py:288
  28.4 7.0 %collective-permute-start.6 = (bf16[256,512]{1,0:T(8,128)(2,1)S(1)}, bf16[256,512]{1,0:T(8,128)(2,1)S(1)}, u32[]{:S(2)}, u32[]{:S(2)}) collective-permute-start(bf16[256,512]{1,0:T(8,128)(2,1)S(1)} %get-tuple-element.29), channel_id=1, source_target_pairs={{0,4},{8,12},{16,20},{24,28},{4,0},{12,8},{20,16},{28,24},{1,5},{9... | collective-permute-start | bytes 786440 | tf_op jit(solution)/shard_map/ppermute | solution.py:192
  30.5 9.2 %collective-permute-start.7 = (bf16[256,512]{1,0:T(8,128)(2,1)S(1)}, bf16[256,512]{1,0:T(8,128)(2,1)S(1)}, u32[]{:S(2)}, u32[]{:S(2)}) collective-permute-start(bf16[256,512]{1,0:T(8,128)(2,1)S(1)} %get-tuple-element.30), channel_id=1, source_target_pairs={{4,8},{12,16},{20,24},{8,4},{16,12},{24,20},{5,9},{13,17},{21,25},... | collective-permute-start | bytes 786440 | tf_op jit(solution)/shard_map/ppermute | solution.py:192
  33.4 1.9 %collective-permute-start.14 = (bf16[128,256]{1,0:T(8,128)(2,1)S(1)}, bf16[128,256]{1,0:T(8,128)(2,1)S(1)}, u32[]{:S(2)}, u32[]{:S(2)}) collective-permute-start(bf16[128,256]{1,0:T(8,128)(2,1)S(1)} %add_convert_fusion.own_field), channel_id=1, source_target_pairs={{0,1},{1,0},{2,3},{3,2},{4,5},{5,4},{6,7},{7,6},{8,9},{9,8},{10,11... | collective-permute-start | bytes 196616 | tf_op jit(solution)/shard_map/ppermute | solution.py:175
